TPU v7x, 512 devices: a whole 4x4x16 slice. The times are simulated.
512 devices in a mesh: dp: 32 (over z_lo, y), tensor: 16 (over z_hi, x, core).
Axes of the slice: x: 4, y: 4, z: 16 (z_hi: 2, z_lo: 8; z = z_hi * 8 + z_lo), core: 2. Of those that a mesh axis runs over, the one named last changes fastest.
Arguments:
- hidden: bfloat16 [8192, 8192], P('dp'), may hold values from -6 to 6
- norm_gain: float32 [8192], replicated, may hold values from 0.1 to 1.9
- w_query: bfloat16 [8192, 4096], P('dp', 'tensor'), may hold values from -0.0447466 to 0.0447466
- w_key: bfloat16 [8192, 512], P('dp', 'tensor'), may hold values from -0.0447466 to 0.0447466
- w_value: bfloat16 [8192, 512], P('dp', 'tensor'), may hold values from -0.0625 to 0.0625
- grad_context: bfloat16 [8192, 4096], P('dp', 'tensor'), may hold values from -6 to 6
Outputs:
- grad_hidden: bfloat16 [8192, 8192], P(('dp', 'tensor'))
All inputs are finite; a program needn't handle non-finite values.
Results may differ from a plain program's by a relative error of at most 0.023.
Values may be sent and summed in bfloat16 or wider, within the bound.
A program may use at most 64 MiB of HBM per device.

v0:
```python
import math

import jax
import jax.numpy as jnp
from jax import lax
from jax.sharding import PartitionSpec as P

KVH = 4
HD = 128


rope_theta = 500000.0


def from_partner(value, axis, distance):
    mask = 2**distance
    pairs = [(source, source ^ mask) for source in range(lax.axis_size(axis))]
    return lax.ppermute(value, axis, pairs)


def as_sent(value):

    def short(part):
        return part.astype(jnp.bfloat16) if part.dtype == jnp.float32 else part

    return jax.tree.map(short, value)


def rotate(values, col_start, direction, head_size):
    row_count = values.shape[0]
    col_count = values.shape[1]
    paired = values.reshape(row_count, col_count // 2, 2)
    even_part = paired[:, :, 0]
    odd_part = paired[:, :, 1]
    columns = col_start + 2 * jnp.arange(col_count // 2, dtype=jnp.int32)
    pair_index = (columns % head_size // 2).astype(jnp.float32)
    frequency = jnp.exp(pair_index * (-2.0 * math.log(rope_theta) / head_size))
    angles = (
        jnp.arange(row_count, dtype=jnp.int32).astype(jnp.float32)[:, None] * frequency[None, :]
    )
    cosine = jnp.cos(angles)
    sine_part = direction * jnp.sin(angles)
    return jnp.stack(
        [even_part * cosine - odd_part * sine_part, even_part * sine_part + odd_part * cosine], -1
    ).reshape(row_count, col_count)


def transposed(left, right):
    return jnp.einsum("sc,dc->sd", left, right, preferred_element_type=jnp.float32)


def per_device(hidden, norm_gain, w_query, w_key, w_value, grad_context):
    tensor_count = lax.axis_size("tensor")
    tensor_rank = lax.axis_index("tensor")
    head_size = HD
    query_cols = w_query.shape[1]
    key_cols = w_key.shape[1]
    local_heads = query_cols // head_size
    share_count = tensor_count // KVH
    level_count = share_count.bit_length() - 1
    hidden_f = hidden.astype(jnp.float32)
    inverse = lax.rsqrt(jnp.mean(hidden_f * hidden_f, axis=1, keepdims=True) + 1e-05)
    gathered = (hidden_f * inverse * norm_gain).astype(jnp.bfloat16)
    seq_len = gathered.shape[0]
    own_rows = seq_len // tensor_count
    pieces = (
        lax.all_gather(w_query, "dp", axis=0, tiled=True),
        lax.all_gather(w_key, "dp", axis=0, tiled=True),
        lax.all_gather(w_value, "dp", axis=0, tiled=True),
    )
    query_sum = jnp.dot(gathered, pieces[0], preferred_element_type=jnp.float32)
    key_sum = jnp.dot(gathered, pieces[1], preferred_element_type=jnp.float32)
    value_sum = jnp.dot(gathered, pieces[2], preferred_element_type=jnp.float32)
    query_b = rotate(query_sum, tensor_rank * query_cols, 1.0, head_size).astype(jnp.bfloat16)
    key_b = rotate(key_sum, tensor_rank * key_cols, 1.0, head_size).astype(jnp.bfloat16)
    value_b = value_sum.astype(jnp.bfloat16)
    joined = jnp.stack([key_b, value_b])
    for bit_index in range(level_count):
        part_width = joined.shape[2]
        flat_rows = joined.size // 128
        incoming = from_partner(joined.reshape(flat_rows, 128), "tensor", bit_index).reshape(
            2, seq_len, part_width
        )
        upper_side = tensor_rank // (1 << bit_index) % 2 == 1
        lower_part = jnp.where(upper_side, incoming, joined)
        upper_part = jnp.where(upper_side, joined, incoming)
        joined = jnp.concatenate([lower_part, upper_part], 2)
    key_head = joined[0]
    value_head = joined[1]
    query_heads = query_b.reshape(seq_len, local_heads, head_size)
    grad_heads = grad_context.reshape(seq_len, local_heads, head_size)
    scale = 1.0 / math.sqrt(head_size)
    scores = (
        jnp.einsum("qhd,kd->hqk", query_heads, key_head, preferred_element_type=jnp.float32) * scale
    )
    positions = jnp.arange(seq_len, dtype=jnp.int32)
    causal = positions[:, None] >= positions[None, :]
    scores = jnp.where(causal[None], scores, jnp.float32(-1e30))
    peak = jnp.max(scores, axis=-1, keepdims=True)
    weights = jnp.exp(scores - peak)
    probs = weights / jnp.sum(weights, axis=-1, keepdims=True)
    probs_b = probs.astype(jnp.bfloat16)
    grad_probs = jnp.einsum(
        "qhd,kd->hqk", grad_heads, value_head, preferred_element_type=jnp.float32
    )
    delta = jnp.sum(probs * grad_probs, axis=-1, keepdims=True)
    grad_scores = (probs * (grad_probs - delta) * scale).astype(jnp.bfloat16)
    grad_query = jnp.einsum(
        "hqk,kd->qhd", grad_scores, key_head, preferred_element_type=jnp.float32
    ).reshape(seq_len, query_cols)
    grad_query_b = rotate(grad_query, tensor_rank * query_cols, -1.0, head_size).astype(
        jnp.bfloat16
    )
    grad_key = rotate(
        jnp.einsum("hqk,qhd->kd", grad_scores, query_heads, preferred_element_type=jnp.float32),
        0,
        -1.0,
        head_size,
    )
    grad_value = jnp.einsum("hqk,qhd->kd", probs_b, grad_heads, preferred_element_type=jnp.float32)
    summed = jnp.stack([grad_key, grad_value])
    for bit_index in range(level_count):
        flat_rows = summed.size // 128
        incoming = from_partner(
            as_sent(summed.reshape(flat_rows, 128)), "tensor", bit_index
        ).reshape(2, seq_len, head_size)
        summed = summed + incoming
    own_start = tensor_rank % share_count * key_cols
    grad_key_b = lax.dynamic_slice_in_dim(summed[0], own_start, key_cols, 1).astype(jnp.bfloat16)
    grad_value_b = lax.dynamic_slice_in_dim(summed[1], own_start, key_cols, 1).astype(jnp.bfloat16)
    pieces = (
        lax.all_gather(w_query, "dp", axis=0, tiled=True),
        lax.all_gather(w_key, "dp", axis=0, tiled=True),
        lax.all_gather(w_value, "dp", axis=0, tiled=True),
    )
    term = (
        transposed(grad_query_b, pieces[0])
        + transposed(grad_key_b, pieces[1])
        + transposed(grad_value_b, pieces[2])
    )
    grad_normed = lax.psum_scatter(
        term.astype(jnp.bfloat16), "tensor", scatter_dimension=0, tiled=True
    ).astype(jnp.float32)
    row_start = tensor_rank * own_rows
    hidden_own = lax.dynamic_slice_in_dim(hidden_f, row_start, own_rows, 0)
    inverse_own = lax.dynamic_slice_in_dim(inverse, row_start, own_rows, 0)
    scaled = grad_normed * norm_gain
    mean_term = jnp.mean(scaled * hidden_own, axis=1, keepdims=True)
    result = inverse_own * (scaled - hidden_own * inverse_own * inverse_own * mean_term)
    return result.astype(jnp.bfloat16)


def solution(mesh):
    in_specs = (
        P("dp", None),
        P(),
        P("dp", "tensor"),
        P("dp", "tensor"),
        P("dp", "tensor"),
        P("dp", "tensor"),
    )
    out_specs = P(("dp", "tensor"), None)
    return jax.shard_map(
        per_device, mesh=mesh, in_specs=in_specs, out_specs=out_specs, check_vma=False
    )
```

profile of v0, /device:TPU:1, one launch (start us, length us, event | category | flops | bytes accessed | tf_op | source)
XLA Modules:
  0.0 462.5 jit_solution(18435431642337077442)
XLA Ops:
  6.5 0.0 all-gather.2.cloned.1.call-start
  6.5 0.7 all-gather.2.cloned.1.call-update
  7.3 0.0 reduce-scatter.2.cloned.1.call-start
  7.3 3.1 multiply_reduce_fusion
  10.4 117.4 %all_gather.12 = bf16[8192,32]{0,1:T(8,128)(2,1)S(1)} all-gather(bf16[256,32]{0,1:T(8,128)(2,1)} %param.9), channel_id=1, replica_groups=mesh['dp'=32,'tensor'=16] {'dp'}, dimensions={0}, use_global_device_ids=true | all-gather | bytes 540672 | tf_op jit(solution)/shard_map/all_gather | solution.py:68
  127.8 3.7 fusion.86
  131.6 0.1 fusion.57
  131.8 103.0 %all_gather.13 = bf16[8192,32]{0,1:T(8,128)(2,1)S(1)} all-gather(bf16[256,32]{0,1:T(8,128)(2,1)S(1)} %copy-done.2), channel_id=1, replica_groups=mesh['dp'=32,'tensor'=16] {'dp'}, dimensions={0}, use_global_device_ids=true | all-gather | bytes 540672 | tf_op jit(solution)/shard_map/all_gather | solution.py:69
  234.8 3.6 fusion.11
  238.4 0.1 copy.59
  238.6 0.1 reshape.538
  238.7 25.3 %collective-permute-start = (bf16[128,128]{1,0:T(8,128)(2,1)S(1)}, bf16[128,128]{1,0:T(8,128)(2,1)S(1)}, u32[]{:S(2)}, u32[]{:S(2)}) collective-permute-start(bf16[128,128]{1,0:T(8,128)(2,1)S(1)} %reshape.538), channel_id=1, source_target_pairs={{0,1},{1,0},{2,3},{3,2},{4,5},{5,4},{6,7},{7,6},{8,9},{9,8},{10,11... | collective-permute-start | bytes 98312 | tf_op jit(solution)/shard_map/ppermute | solution.py:18
  264.2 0.1 copy.101
  264.3 0.6 collective-permute-done
  264.9 0.1 reshape.539
  265.0 0.1 copy.60
  265.1 0.1 copy.62
  265.2 0.1 reshape.540
  265.4 3.2 collective-permute-start.1
  268.6 1.8 collective-permute-done.1
  270.4 0.1 reshape.541
  270.5 0.1 copy.63
  270.6 0.2 convolution_bitcast_fusion
  270.9 0.0 all-gather.2.cloned.1.call-done
  270.9 5.5 %fusion.85 = f32[256,256]{0,1:T(8,128)S(1)} fusion(bf16[8192,256]{1,0:T(8,128)(2,1)} %all-gather.2.cloned.1.call-done, f32[8192]{0:T(1024)S(1)} %copy-done, f32[256]{0:T(256)S(1)} %add_rsqrt_fusion, bf16[256,8192]{1,0:T(8,128)(2,1)} %param.6), kind=kOutput, calls=%fused_computation.136 | convolution fusion | flops 1082130432 | bytes 8684544 | tf_op jit(solution)/shard_map/dot_general | solution.py:71
  276.5 0.1 reshape.542
  276.6 0.2 fusion.88
  276.8 0.1 copy.98
  276.9 0.1 copy.97
  277.0 0.6 fusion.37
  277.6 0.1 copy.67
  277.8 0.1 convert_element_type.142
  277.9 0.1 copy.76
  278.0 0.4 fusion.91
  278.4 0.6 convolution_bitcast_fusion.2
  278.9 0.3 convolution_bitcast_fusion.1
  279.2 0.3 convolution_bitcast_fusion.3
  279.5 0.3 fusion.42
  279.9 0.1 copy.79
  280.0 0.1 stack_reshape.3
  280.1 0.1 reshape_reshape.3
  280.3 0.2 fusion.87
  280.5 0.1 copy.100
  280.6 0.1 copy.99
  280.7 0.1 copy.82
  280.9 3.4 collective-permute-start.2
  284.3 0.6 fusion.34
  284.9 0.1 copy.75
  285.0 0.1 convert_element_type.144
  285.1 0.1 collective-permute-done.2
  285.3 3.3 collective-permute-start.3
  288.6 6.7 %fusion.94 = f32[256,8192]{1,0:T(8,128)} fusion(bf16[256,256]{0,1:T(8,128)(2,1)S(1)} %convert_element_type.144, bf16[8192,256]{1,0:T(8,128)(2,1)} %all-gather.2.cloned.1.call-done), kind=kOutput, calls=%fused_computation.143 | convolution fusion | flops 1073741824 | bytes 12713984 | tf_op jit(solution)/shard_map/sc,dc->sd/dot_general | solution.py:49
  295.3 0.1 copy.83
  295.5 0.0 collective-permute-done.3
  295.5 0.1 copy.84
  295.6 0.1 add_add_fusion
  295.7 4.7 %convolution_add_fusion.1 = f32[256,8192]{1,0:T(8,128)S(1)} fusion(f32[256,8192]{1,0:T(8,128)} %fusion.94, bf16[8192,32]{0,1:T(8,128)(2,1)S(1)} %all_gather.12, bf16[1,256,128]{1,2,0:T(8,128)(2,1)S(1)} %get-tuple-element.16, s32[]{:T(128)S(6)} %select_n.146), kind=kOutput, calls=%fused_computation.3 | convolution fusion | flops 136314880 | bytes 17317892 | tf_op jit(solution)/shard_map/sc,dc->sd/dot_general | solution.py:49
  300.3 3.3 fusion.2
  303.6 0.0 reduce-scatter.2.cloned.1.call-update
  303.6 6.4 %convert_element_type.134 = f32[256,8192]{1,0:T(8,128)} convert(bf16[256,8192]{1,0:T(8,128)(2,1)} %param.6) | non-fusion elementwise | flops 2097152 | bytes 12582912 | tf_op jit(solution)/shard_map/convert_element_type | solution.py:61
  310.0 0.1 dynamic-slice.5
  310.1 142.2 %reduce-scatter.2.cloned.1.call-done = bf16[16,8192]{1,0:T(8,128)(2,1)} async-done(((bf16[256,8192]{1,0:T(8,128)(2,1)}), bf16[16,8192]{1,0:T(8,128)(2,1)}) %reduce-scatter.2.cloned.1.call-update) | async-done | bytes 262160 | tf_op jit(solution)/shard_map/reduce_scatter | solution.py:141
  452.3 1.3 multiply_reduce_fusion.1
  453.6 2.0 multiply_convert_fusion.1
  (29 shorter events, 0.4 us)
Async XLA Ops:
  6.5 228.3 %copy-start = (f32[8192]{0:T(1024)S(1)}, f32[8192]{0:T(1024)}, u32[]{:S(2)}) copy-start(f32[8192]{0:T(1024)} %param.7) | copy-start | bytes 98308
  6.5 125.2 %copy-start.2 = (bf16[256,32]{0,1:T(8,128)(2,1)S(1)}, bf16[256,32]{0,1:T(8,128)(2,1)}, u32[]{:S(2)}) copy-start(bf16[256,32]{0,1:T(8,128)(2,1)} %param.10) | copy-start | bytes 49156
  6.5 264.4 %all-gather.2.cloned.1.call-start = ((), (), s32[]{:S(2)}) async-start(), calls=%async_computation.1 | async-start | bytes 4325376 | tf_op jit(solution)/shard_map/all_gather | solution.py:67
  7.3 445.1 %reduce-scatter.2.cloned.1.call-start = ((), (), s32[]{:S(2)}) async-start(), calls=%async_computation.2 | async-start | bytes 4456448 | tf_op jit(solution)/shard_map/reduce_scatter | solution.py:141
  127.8 136.4 %copy-start.1 = (bf16[256,256]{1,0:T(8,128)(2,1)S(1)}, bf16[256,256]{1,0:T(8,128)(2,1)}, u32[]{:S(2)}) copy-start(bf16[256,256]{1,0:T(8,128)(2,1)} %param.11) | copy-start | bytes 393220
  238.7 26.2 %collective-permute-start = (bf16[128,128]{1,0:T(8,128)(2,1)S(1)}, bf16[128,128]{1,0:T(8,128)(2,1)S(1)}, u32[]{:S(2)}, u32[]{:S(2)}) collective-permute-start(bf16[128,128]{1,0:T(8,128)(2,1)S(1)} %reshape.538), channel_id=1, source_target_pairs={{0,1},{1,0},{2,3},{3,2},{4,5},{5,4},{6,7},{7,6},{8,9},{9,8},{10,11... | collective-permute-start | bytes 98312 | tf_op jit(solution)/shard_map/ppermute | solution.py:18
  265.4 5.0 %collective-permute-start.1 = (bf16[256,128]{1,0:T(8,128)(2,1)S(1)}, bf16[256,128]{1,0:T(8,128)(2,1)S(1)}, u32[]{:S(2)}, u32[]{:S(2)}) collective-permute-start(bf16[256,128]{1,0:T(8,128)(2,1)S(1)} %reshape.540), channel_id=1, source_target_pairs={{0,2},{1,3},{2,0},{3,1},{4,6},{5,7},{6,4},{7,5},{8,10},{9,11},{10,... | collective-permute-start | bytes 196616 | tf_op jit(solution)/shard_map/ppermute | solution.py:18
  280.9 4.4 collective-permute-start.2
  285.3 10.2 %collective-permute-start.3 = (bf16[512,128]{1,0:T(8,128)(2,1)S(1)}, bf16[512,128]{1,0:T(8,128)(2,1)S(1)}, u32[]{:S(2)}, u32[]{:S(2)}) collective-permute-start(bf16[512,128]{1,0:T(8,128)(2,1)S(1)} %fusion.13), channel_id=1, source_target_pairs={{0,2},{1,3},{2,0},{3,1},{4,6},{5,7},{6,4},{7,5},{8,10},{9,11},{10,... | collective-permute-start | bytes 393224 | tf_op jit(solution)/shard_map/ppermute | solution.py:18
Sparse Core Ops, SparseCore 0:
  9.4 215.0 all-gather.1
  303.8 148.5 reduce-scatter.1
where the time goes:
time: 464 us; the launch traced here: 462 us
  blocking collectives  220 us (47%)
  waiting for transfers between devices  146 us (31%)
  starting transfers between devices  35.3 us (8%)
  matrix products  29.2 us (6%)
  other arithmetic  14.8 us (3%)
  between operations  13.9 us (3%)
    reduce_scatter x1, waiting for transfers between devices, per_device(): lax.psum_scatter(term.astype(jnp.bfloat16), 'tensor', scatter_dimension=0...  142 us
    all_gather x1, blocking collectives, per_device(): lax.all_gather(w_key, 'dp', axis=0, tiled=True)  117 us
    all_gather x1, blocking collectives, per_device(): lax.all_gather(w_value, 'dp', axis=0, tiled=True)  103 us
    ppermute x4, starting transfers between devices, from_partner(): return lax.ppermute(value, axis, pairs)  35.3 us
    dot_general x3, matrix products, transposed(): jnp.einsum('sc,dc->sd', left, right, preferred_element_type=jnp.float32)  14.6 us
  transfers between devices with their start and end apart: 6, of which 4 were waited for; matrix products, arithmetic and copies ran while one was open for 6% of the time, Pallas kernels for 0%

commit v1 on v0

v1 whole, which is shorter than its diff:
```python
import functools
import math

import jax
import jax.numpy as jnp
import numpy as np
from jax import lax
from jax.experimental import pallas as pl
from jax.experimental.pallas import tpu as pltpu
from jax.sharding import PartitionSpec as P

D = 8192
HD = 128
SEQ = 256
NZ, NY, NX = 8, 4, 4
SLOTS = NZ * NY
ROWS = 640
HALF = ROWS // 2
ROPE_THETA = 500000.0
SCALE = 1.0 / math.sqrt(HD)
MESH = pl.DeviceIdType.MESH
F32, BF16 = jnp.float32, jnp.bfloat16


def rotary_tables():
    lane = np.arange(HD)
    frequency = np.exp((lane // 2) * (-2.0 * math.log(ROPE_THETA) / HD))
    angle = np.arange(SEQ)[:, None] * frequency[None, :]
    cosine = np.cos(angle)
    sine = np.sin(angle) * np.where(lane % 2 == 0, -1.0, 1.0)[None, :]
    packed_cos = np.ones((4, 128, 128))
    packed_sin = np.zeros((4, 128, 128))
    for rank in range(4):
        columns = slice(32 * rank, 32 * rank + 32)
        for part in range(2):
            rows = slice(128 * part, 128 * part + 128)
            packed_cos[rank, :, 64 * part : 64 * part + 32] = cosine[rows, columns]
            packed_sin[rank, :, 64 * part : 64 * part + 32] = sine[rows, columns]
    return [table.astype(np.float32) for table in (cosine, sine, packed_cos, packed_sin)]


def dot(left, right):
    return lax.dot_general(left, right, (((1,), (0,)), ((), ())), preferred_element_type=F32)


def dot_rows(left, right):
    return lax.dot_general(left, right, (((1,), (1,)), ((), ())), preferred_element_type=F32)


def dot_columns(left, right):
    return lax.dot_general(left, right, (((0,), (0,)), ((), ())), preferred_element_type=F32)


def lanes_of(value):
    return lax.broadcasted_iota(jnp.int32, value.shape, 1)


def rotate(value, cosine, sine):
    left = pltpu.roll(value, 127, 1)
    right = pltpu.roll(value, 1, 1)
    swapped = jnp.where(lanes_of(value) % 2 == 0, left, right)
    return value * cosine + swapped * sine


def kernel(
    hid_ref, gain_ref, wq_ref, wk_ref, wv_ref, gc_ref, cos_ref, sin_ref, kcos_ref, ksin_ref,
    out_ref,
    hid, W, N, qacc, kvacc, kvs, dks, dkr, A,
    sibs, sibr, own, S, xrelay, xin, fs, zsend, zin, G,
    hid_sem, load_sem, ag_recv, ag_send, kv_recv, kv_send, dk_recv, dk_send,
    sib_recv, sib_send, x_recv, x_send, z_recv, z_send,
):
    dp = lax.axis_index("dp")
    tensor = lax.axis_index("tensor")
    z, y = dp // NY, dp % NY
    zh, x, c = tensor // 8, (tensor // 2) % NX, tensor % 2
    rank = tensor % 4
    yl, yr, yo = (y + 3) % 4, (y + 1) % 4, (y + 2) % 4
    xl, xr, xo = (x + 3) % 4, (x + 1) % 4, (x + 2) % 4

    def at_dp(zz, yy):
        return (zz * NY + yy, tensor)

    def at_tensor(zhh, xx, cc):
        return (dp, zhh * 8 + xx * 2 + cc)

    up, down = at_dp(z + 1, y), at_dp(z - 1, y)
    to_yl, to_yr = at_dp(z, yl), at_dp(z, yr)
    to_xl, to_xr = at_tensor(zh, xl, c), at_tensor(zh, xr, c)
    sibling = at_tensor(zh, x, 1 - c)
    far = at_tensor(1 - zh, x, c)
    x_pair = x + 1 - 2 * (x % 2)
    group = {1: sibling, 2: at_tensor(zh, x_pair, c), 3: at_tensor(zh, x_pair, 1 - c)}

    def remote(src, dst, send, recv, device):
        return pltpu.make_async_remote_copy(
            src_ref=src, dst_ref=dst, send_sem=send, recv_sem=recv, device_id=device, device_id_type=MESH
        )

    mine = z * NY + y
    load_q0 = pltpu.make_async_copy(wq_ref.at[:, pl.ds(0, 128)], W.at[mine, pl.ds(0, 256)], load_sem.at[0])
    load_q1 = pltpu.make_async_copy(wq_ref.at[:, pl.ds(128, 128)], W.at[mine, pl.ds(256, 256)], load_sem.at[1])
    load_hid = pltpu.make_async_copy(hid_ref, hid, hid_sem)
    load_q0.start()
    load_q1.start()
    barrier = pltpu.get_barrier_semaphore()

    def greet(device):
        pl.semaphore_signal(barrier, inc=1, device_id=device, device_id_type=MESH)

    for device in (to_yl, to_yr, to_xl, to_xr, sibling, group[3], far):
        greet(device)

    @pl.when(z < NZ - 1)
    def _():
        greet(up)

    @pl.when(z > 0)
    def _():
        greet(down)

    load_hid.start()
    wk, wv = wk_ref[...].astype(F32), wv_ref[...].astype(F32)
    packed = jnp.concatenate([wk[:128], wv[:128], wk[128:], wv[128:]], axis=1)
    W[mine, 512:640, :] = packed.astype(BF16)
    load_q0.wait()
    load_q1.wait()
    pl.semaphore_wait(barrier, 7 + jnp.where(z < NZ - 1, 1, 0) + jnp.where(z > 0, 1, 0))

    def block(i, device, kind):
        return remote(W.at[i], W.at[i], ag_send.at[kind, i], ag_recv.at[i, 0], device)

    def half_block(i, part, device):
        rows = pl.ds(part * HALF, HALF)
        return remote(W.at[i, rows], W.at[i, rows], ag_send.at[3, i], ag_recv.at[i, part], device)

    def plane(n):
        s = (n + 1) // 2
        return jnp.where(n % 2 == 1, z - s, z + s)

    def inside(j):
        return jnp.logical_and(j >= 0, j < NZ)

    def go_up(j):
        return jnp.logical_and(j <= z, z < NZ - 1)

    def go_down(j):
        return jnp.logical_and(j >= z, z > 0)

    def spread(j):
        i = j * NY + y

        @pl.when(go_up(j))
        def _():
            block(i, up, 0).start()

        @pl.when(go_down(j))
        def _():
            block(i, down, 4).start()

        block(i, to_yr, 1).start()
        block(i, to_yl, 2).start()

    def multiply(i):
        columns = pl.ds(pl.multiple_of(i * 256, 256), 256)
        rows = N[:, columns]
        qacc[0] += dot(rows, W[i, 0:256, :])
        qacc[1] += dot(rows, W[i, 256:512, :])
        both = W[i, 512:640, :]
        kvacc[0] += dot(rows[:, 0:128], both)
        kvacc[1] += dot(rows[:, 128:256], both)

    spread(z)
    qacc[...] = jnp.zeros_like(qacc)
    kvacc[...] = jnp.zeros_like(kvacc)
    load_hid.wait()

    def norm_rows(b, carry):
        rows = pl.ds(pl.multiple_of(b * 16, 16), 16)
        values = hid[rows, :].astype(F32)
        inverse = lax.rsqrt(jnp.mean(values * values, axis=1, keepdims=True) + 1e-05)
        N[rows, :] = (values * inverse * gain_ref[...]).astype(BF16)
        return carry

    lax.fori_loop(0, SEQ // 16, norm_rows, 0)

    def gather_step(n, carry):
        ja = plane(n)

        @pl.when(jnp.logical_and(inside(ja), jnp.logical_and(n > 0, n < 15)))
        def _():
            i = ja * NY + y
            block(i, up, 0).wait_recv()
            spread(ja)

        jb = plane(n - 2)

        @pl.when(jnp.logical_and(inside(jb), jnp.logical_and(n >= 2, n < 17)))
        def _():
            i_left, i_right = jb * NY + yl, jb * NY + yr
            block(i_left, to_yr, 1).wait_recv()
            half_block(i_left, 0, to_yr).start()
            block(i_right, to_yl, 2).wait_recv()
            half_block(i_right, 1, to_yl).start()
            multiply(jb * NY + y)
            multiply(i_left)
            multiply(i_right)

        jc = plane(n - 4)

        @pl.when(jnp.logical_and(inside(jc), n >= 4))
        def _():
            i = jc * NY + yo
            half_block(i, 0, to_yr).wait_recv()
            half_block(i, 1, to_yl).wait_recv()
            multiply(i)

        return carry

    lax.fori_loop(0, 19, gather_step, 0)

    lane = lax.broadcasted_iota(jnp.int32, (128, 128), 1)
    kva, kvb = kvacc[0], kvacc[1]
    low = kva[:128] + pltpu.roll(kvb[:128], 64, 1)
    high = pltpu.roll(kva[128:], 64, 1) + kvb[128:]
    kv_own = rotate(jnp.where(lane < 64, low, high), kcos_ref[rank], ksin_ref[rank])
    kvs[rank] = kv_own.astype(BF16)

    def peer(step):
        if step == 1:
            return rank + 1 - 2 * (rank % 2)
        if step == 2:
            return (rank + 2) % 4
        return 3 - rank

    def kv_copy(step):
        return remote(kvs.at[rank], kvs.at[rank], kv_send.at[step - 1], kv_recv.at[step - 1], group[step])

    for step in (1, 2, 3):
        kv_copy(step).start()
    q_heads = []
    for h in range(2):
        q_heads.append(rotate(qacc[h], cos_ref[...], sin_ref[...]).astype(BF16))
    for step in (1, 2, 3):
        kv_copy(step).wait()

    def unpack(shift):
        parts = []
        for part in range(2):
            total = jnp.zeros((128, 128), F32)
            for r in range(4):
                piece = kvs[r].astype(F32)
                amount = (32 * r - shift - 64 * part) % 128
                piece = pltpu.roll(piece, amount, 1) if amount else piece
                total = jnp.where(lane // 32 == r, piece, total)
            parts.append(total)
        return jnp.concatenate(parts, axis=0).astype(BF16)

    k_head, v_head = unpack(0), unpack(32)
    row_id = lax.broadcasted_iota(jnp.int32, (SEQ, SEQ), 0)
    col_id = lax.broadcasted_iota(jnp.int32, (SEQ, SEQ), 1)
    causal = row_id >= col_id
    dk = jnp.zeros((SEQ, HD), F32)
    dv = jnp.zeros((SEQ, HD), F32)
    dq_heads = []
    for h in range(2):
        g_head = gc_ref[:, h * HD : (h + 1) * HD]
        scores = jnp.where(causal, dot_rows(q_heads[h], k_head) * SCALE, -1e30)
        weights = jnp.exp(scores - jnp.max(scores, axis=1, keepdims=True))
        probs = weights / jnp.sum(weights, axis=1, keepdims=True)
        grad_probs = dot_rows(g_head, v_head)
        delta = jnp.sum(probs * grad_probs, axis=1, keepdims=True)
        grad_scores = (probs * (grad_probs - delta) * SCALE).astype(BF16)
        dq = dot(grad_scores, k_head)
        dq_heads.append(rotate(dq, cos_ref[...], -sin_ref[...]).astype(BF16))
        dk = dk + dot_columns(grad_scores, q_heads[h])
        dv = dv + dot_columns(probs.astype(BF16), g_head)

    def pack(r):
        def shifted(value, amount):
            amount = amount % 128
            return pltpu.roll(value, amount, 1) if amount else value

        total = shifted(dk[:128], -32 * r)
        total = jnp.where(lane // 32 == 1, shifted(dv[:128], 32 - 32 * r), total)
        total = jnp.where(lane // 32 == 2, shifted(dk[128:], 64 - 32 * r), total)
        return jnp.where(lane // 32 == 3, shifted(dv[128:], 96 - 32 * r), total)

    for r in range(4):
        dks[r] = pack(r)
    for step in (1, 2, 3):
        dkr[step - 1] = dks[peer(step)].astype(BF16)

    def dk_copy(step):
        return remote(dkr.at[step - 1], dkr.at[step + 2], dk_send.at[step - 1], dk_recv.at[step - 1], group[step])

    for step in (1, 2, 3):
        dk_copy(step).start()

    def ordered(value, core):
        return jnp.concatenate(
            [value[16 * (8 * b + 2 * a + core) : 16 * (8 * b + 2 * a + core) + 16] for a in range(NX) for b in range(2)],
            axis=0,
        )

    def place(value, lanes):
        for core in range(2):
            part = ordered(value, core)
            start = pl.multiple_of(jnp.where(c == core, 128, 0), 128)
            A[pl.ds(start, 128), lanes * 128 : lanes * 128 + 128] = part

    place(dq_heads[0], 0)
    place(dq_heads[1], 1)
    for step in (1, 2, 3):
        dk_copy(step).wait()
    dkv = dks[rank] + dkr[3].astype(F32) + dkr[4].astype(F32) + dkr[5].astype(F32)
    dkv = rotate(dkv, kcos_ref[rank], -ksin_ref[rank])
    turned = pltpu.roll(dkv, 64, 1)
    place(jnp.concatenate([jnp.where(lane < 64, dkv, 0.0), jnp.where(lane < 64, turned, 0.0)], axis=0).astype(BF16), 2)
    place(jnp.concatenate([jnp.where(lane < 64, 0.0, turned), jnp.where(lane < 64, 0.0, dkv)], axis=0).astype(BF16), 3)

    def sib_copy(m):
        return remote(sibs.at[m], sibr.at[m], sib_send.at[m], sib_recv.at[m], sibling)

    def relay_up(m):
        return remote(S.at[m, 0, xo], xrelay.at[m, 0], x_send.at[0, m], x_recv.at[0, m], to_xr)

    def relay_down(m):
        return remote(S.at[m, 1, xo], xrelay.at[m, 1], x_send.at[1, m], x_recv.at[1, m], to_xl)

    def direct_up(m):
        return remote(S.at[m, 1, xr], xin.at[m, 0], x_send.at[2, m], x_recv.at[2, m], to_xr)

    def direct_down(m):
        return remote(S.at[m, 0, xl], xin.at[m, 1], x_send.at[3, m], x_recv.at[3, m], to_xl)

    def summed_up(m):
        return remote(S.at[m, 0, xr], xin.at[m, 2], x_send.at[4, m], x_recv.at[4, m], to_xr)

    def summed_down(m):
        return remote(S.at[m, 1, xl], xin.at[m, 3], x_send.at[5, m], x_recv.at[5, m], to_xl)

    def far_copy(m):
        return remote(zsend.at[m], zin.at[m], z_send.at[m], z_recv.at[m], far)

    def term(m):
        dq = A[:, 0:256]
        dkv_a, dkv_b = A[:, 256:384], A[:, 384:512]
        for k in range(NY):
            i = m * NY + k
            weights = jnp.concatenate([W[i, 0:256, :], W[i, 256:512, :]], axis=1)
            both = W[i, 512:640, :]
            value = dot_rows(dq, weights)
            value = value + jnp.concatenate([dot_rows(dkv_a, both), dot_rows(dkv_b, both)], axis=1)
            columns = slice((k % 2) * 256, (k % 2) * 256 + 256)
            sibs[m, k // 2, :, columns] = value[:128].astype(BF16)
            own[m, k // 2, :, columns] = value[128:]
        sib_copy(m).start()

    def over_cores(m):
        sib_copy(m).wait_recv()
        for h in range(2):
            for a in range(NX):
                rows = slice(32 * a, 32 * a + 32)
                S[m, h, a] = (own[m, h, rows, :] + sibr[m, h, rows, :].astype(F32)).astype(BF16)
        relay_up(m).start()
        relay_down(m).start()
        direct_up(m).start()
        direct_down(m).start()

    def over_x(m):
        relay_up(m).wait_recv()
        S[m, 0, xr] = (S[m, 0, xr].astype(F32) + xrelay[m, 0].astype(F32)).astype(BF16)
        summed_up(m).start()
        relay_down(m).wait_recv()
        S[m, 1, xl] = (S[m, 1, xl].astype(F32) + xrelay[m, 1].astype(F32)).astype(BF16)
        summed_down(m).start()

    def at_owner_x(m):
        direct_up(m).wait_recv()
        direct_down(m).wait_recv()
        summed_up(m).wait_recv()
        summed_down(m).wait_recv()
        for h in range(2):
            first, second = (1, 2) if h == 0 else (0, 3)
            total = S[m, h, x].astype(F32) + xin[m, first].astype(F32) + xin[m, second].astype(F32)
            fs[m, 0, h] = total[0:16]
            fs[m, 1, h] = total[16:32]
        zsend[m] = fs[m, 1 - zh].astype(BF16)
        far_copy(m).start()

    own_rows = pl.ds(pl.multiple_of(tensor * 16, 16), 16)

    def columns_of(m, h):
        return pl.ds(pl.multiple_of(m * 1024 + h * 512, 512), 512)

    def at_owner(m, dots):
        far_copy(m).wait_recv()
        for h in range(2):
            columns = columns_of(m, h)
            scaled = (fs[m, zh, h] + zin[m, h].astype(F32)) * gain_ref[:, columns]
            G[m, h] = scaled
            dots = dots + scaled * hid[own_rows, columns].astype(F32)
        return dots

    def sum_step(n, dots):
        @pl.when(n < NZ)
        def _():
            term(n)

        @pl.when(jnp.logical_and(n >= 1, n < NZ + 1))
        def _():
            over_cores(n - 1)

        @pl.when(jnp.logical_and(n >= 2, n < NZ + 2))
        def _():
            over_x(n - 2)

        @pl.when(n >= 3)
        def _():
            at_owner_x(n - 3)

        return dots

    lax.fori_loop(0, NZ + 3, sum_step, 0)
    dots = lax.fori_loop(0, NZ, at_owner, jnp.zeros((16, 512), F32))
    mean_term = jnp.sum(dots, axis=1, keepdims=True) * (1.0 / D)
    own_hidden = hid[own_rows, :].astype(F32)
    inverse = lax.rsqrt(jnp.mean(own_hidden * own_hidden, axis=1, keepdims=True) + 1e-05)
    factor = inverse * inverse * mean_term
    for m in range(NZ):
        for h in range(2):
            columns = slice(m * 1024 + h * 512, m * 1024 + h * 512 + 512)
            value = inverse * (G[m, h] - own_hidden[:, columns] * factor)
            out_ref[:, columns] = value.astype(BF16)

    def gather_sent(j, carry):
        i = j * NY + y

        @pl.when(go_up(j))
        def _():
            block(i, up, 0).wait_send()

        @pl.when(go_down(j))
        def _():
            block(i, down, 4).wait_send()

        block(i, to_yr, 1).wait_send()
        block(i, to_yl, 2).wait_send()
        half_block(j * NY + yl, 0, to_yr).wait_send()
        half_block(j * NY + yr, 1, to_yl).wait_send()
        return carry

    lax.fori_loop(0, NZ, gather_sent, 0)

    def sum_sent(m, carry):
        for copy in (sib_copy, relay_up, relay_down, direct_up, direct_down, summed_up, summed_down, far_copy):
            copy(m).wait_send()
        return carry

    lax.fori_loop(0, NZ, sum_sent, 0)


def per_device(hidden, norm_gain, w_query, w_key, w_value, grad_context):
    tables = [jnp.asarray(table) for table in rotary_tables()]
    vmem = pl.BlockSpec(memory_space=pltpu.VMEM)
    hbm = pl.BlockSpec(memory_space=pl.ANY)
    dma = pltpu.SemaphoreType.DMA
    return pl.pallas_call(
        kernel,
        out_shape=jax.ShapeDtypeStruct((16, D), BF16),
        in_specs=[hbm, vmem, hbm, vmem, vmem, vmem, vmem, vmem, vmem, vmem],
        out_specs=vmem,
        scratch_shapes=[
            pltpu.VMEM((SEQ, D), BF16),
            pltpu.VMEM((SLOTS, ROWS, 128), BF16),
            pltpu.VMEM((SEQ, D), BF16),
            pltpu.VMEM((2, SEQ, HD), F32),
            pltpu.VMEM((2, SEQ, HD), F32),
            pltpu.VMEM((4, 128, 128), BF16),
            pltpu.VMEM((4, 128, 128), F32),
            pltpu.VMEM((6, 128, 128), BF16),
            pltpu.VMEM((SEQ, 512), BF16),
            pltpu.VMEM((NZ, 2, 128, 512), BF16),
            pltpu.VMEM((NZ, 2, 128, 512), BF16),
            pltpu.VMEM((NZ, 2, 128, 512), F32),
            pltpu.VMEM((NZ, 2, NX, 32, 512), BF16),
            pltpu.VMEM((NZ, 2, 32, 512), BF16),
            pltpu.VMEM((NZ, 4, 32, 512), BF16),
            pltpu.VMEM((NZ, 2, 2, 16, 512), F32),
            pltpu.VMEM((NZ, 2, 16, 512), BF16),
            pltpu.VMEM((NZ, 2, 16, 512), BF16),
            pltpu.VMEM((NZ, 2, 16, 512), F32),
            dma,
            dma((2,)),
            dma((SLOTS, 2)),
            dma((5, SLOTS)),
            dma((3,)),
            dma((3,)),
            dma((3,)),
            dma((3,)),
            dma((NZ,)),
            dma((NZ,)),
            dma((6, NZ)),
            dma((6, NZ)),
            dma((NZ,)),
            dma((NZ,)),
        ],
        compiler_params=pltpu.CompilerParams(
            collective_id=0, has_side_effects=True, vmem_limit_bytes=48 * 1024 * 1024
        ),
        name="attention_input_grad",
    )(hidden, norm_gain.reshape(1, D), w_query, w_key, w_value, grad_context, *tables)


def solution(mesh):
    in_specs = (
        P("dp", None),
        P(),
        P("dp", "tensor"),
        P("dp", "tensor"),
        P("dp", "tensor"),
        P("dp", "tensor"),
    )
    out_specs = P(("dp", "tensor"), None)
    return jax.shard_map(
        per_device, mesh=mesh, in_specs=in_specs, out_specs=out_specs, check_vma=False
    )
```

time: 464 us -> 126 us (0.27)
  blocking collectives: 220 us -> 0 us
  waiting for transfers between devices: 146 us -> 0 us
  Pallas kernels: 0 us -> 115 us
  starting transfers between devices: 35.3 us -> 0 us
  matrix products: 29.2 us -> 0 us
  other arithmetic: 14.8 us -> 0 us
  between operations: 13.9 us -> 0.03 us
  local copies, waits for them, and re-layouts: 3.33 us -> 10.8 us
    all_gather x2 -> x0, blocking collectives: 220 us -> none  [the longest x1 117 us: per_device(): lax.all_gather(w_key, 'dp', axis=0, tiled=True)]
    reduce_scatter x1 -> x0, waiting for transfers between devices: 142 us -> none  [per_device(): lax.psum_scatter(term.astype(jnp.bfloat16), 'tensor', scatter_dimension=0...]
    pallas_call x0 -> x1, Pallas kernels: none -> 115 us  [per_device(): pl.pallas_call(kernel, out_shape=jax.ShapeDtypeStruct((16, D), BF16), in_...]
    ppermute x4 -> x0, starting transfers between devices: 35.3 us -> none  [from_partner(): return lax.ppermute(value, axis, pairs)]
    dot_general x10 -> x0, matrix products: 28.9 us -> none  [the longest x3 14.6 us: transposed(): jnp.einsum('sc,dc->sd', left, right, preferred_element_type=jnp.float32)]
    unnamed x10 -> x19, local copies, waits for them, and re-layouts: 0.4 us -> 10.8 us
    convert_element_type x6 -> x0, other arithmetic: 8.47 us -> none  [the longest x1 6.4 us: per_device(): hidden_f = hidden.astype(jnp.float32)]
  transfers between devices with their start and end apart: 6 -> 0, of which waited for: 4 -> 0; matrix products, arithmetic and copies ran while one was open for 6% -> 0% of each run, Pallas kernels for 0% -> 0%
where the time goes in v1:
time: 126 us
  Pallas kernels  115 us (91%)
  local copies, waits for them, and re-layouts  10.8 us (9%)
    pallas_call x1, Pallas kernels, per_device(): pl.pallas_call(kernel, out_shape=jax.ShapeDtypeStruct((16, D), BF16), in_...  115 us
    unnamed x19, local copies, waits for them, and re-layouts  10.8 us

profile of v1, /device:TPU:1, one launch (start us, length us, event | category | flops | bytes accessed | tf_op | source)
XLA Modules:
  0.0 125.8 jit_solution(4664959576617381122)
XLA Ops:
  0.0 0.8 copy.11.wk_ref
  0.8 0.8 copy.12.wv_ref
  1.7 0.0 copy-start
  1.7 2.2 %copy-done = bf16[256,8192]{1,0:T(8,128)(2,1)S(1)} copy-done((bf16[256,8192]{1,0:T(8,128)(2,1)S(1)}, bf16[256,8192]{1,0:T(8,128)(2,1)}, u32[]{:S(2)}) %copy-start) | copy-done | bytes 4194328
  3.9 0.0 copy-start.1
  3.9 0.9 copy-done.1
  4.8 0.0 copy-start.2
  4.8 0.9 copy-done.2
  5.8 0.0 copy-start.3
  5.8 0.9 copy-done.3
  6.7 0.0 copy-start.4
  6.7 0.9 copy-done.4
  7.6 0.0 copy-start.5
  7.6 0.9 copy-done.5
  8.5 0.0 copy-start.6
  8.5 0.9 copy-done.6
  9.4 0.0 copy-start.7
  9.4 0.8 copy-done.7
  10.1 115.0 %attention_input_grad.1 = bf16[16,8192]{1,0:T(8,128)(2,1)S(1)} custom-call(bf16[256,8192]{1,0:T(8,128)(2,1)S(1)} %copy-done, f32[1,8192]{1,0:T(1,128)S(1)} %bitcast.1, bf16[256,256]{1,0:T(8,128)(2,1)S(1)} %copy-done.3, bf16[256,32]{1,0:T(8,128)(2,1)S(1)} %copy.11.wk_ref, bf16[256,32]{1,0:T(8,128)(2,1)S(1)} %copy.12.wv_ref, bf16[256,256]{1,0:T(8,128)(2,1)S(1)} %copy-done.4, ...), custom_call_target="tpu_custom_call" | custom-call | tf_op jit(solution)/shard_map/attention_input_grad/pallas_call | solution.py:469
  125.1 0.7 copy.14
Async XLA Ops:
  1.7 2.2 %copy-start = (bf16[256,8192]{1,0:T(8,128)(2,1)S(1)}, bf16[256,8192]{1,0:T(8,128)(2,1)}, u32[]{:S(2)}) copy-start(bf16[256,8192]{1,0:T(8,128)(2,1)} %hid_ref.1) | copy-start | bytes 12582916
  3.9 0.9 copy-start.1
  4.8 0.9 copy-start.2
  5.8 0.9 copy-start.3
  6.7 0.9 copy-start.4
  7.6 0.9 copy-start.5
  8.5 0.9 copy-start.6
  9.4 0.8 copy-start.7

commit v2 on v1

--- a/solution.py
+++ b/solution.py
@@ -15,7 +15,9 @@
 NZ, NY, NX = 8, 4, 4
 SLOTS = NZ * NY
 ROWS = 640
-HALF = ROWS // 2
+PARTS = 4
+PART = ROWS // PARTS
+LAG_B, LAG_C = 3, 8
 ROPE_THETA = 500000.0
 SCALE = 1.0 / math.sqrt(HD)
 MESH = pl.DeviceIdType.MESH
@@ -63,11 +65,11 @@
 
 
 def kernel(
-    hid_ref, gain_ref, wq_ref, wk_ref, wv_ref, gc_ref, cos_ref, sin_ref, kcos_ref, ksin_ref,
+    hid_hbm, gain_hbm, wq_hbm, wk_hbm, wv_hbm, gc_hbm, cos_hbm, sin_hbm, kcos_hbm, ksin_hbm,
     out_ref,
-    hid, W, N, qacc, kvacc, kvs, dks, dkr, A,
+    hid, gain, wkv, gc, cosine, sine, kcos, ksin, W, N, qacc, kvacc, kvs, dks, dkr, A,
     sibs, sibr, own, S, xrelay, xin, fs, zsend, zin, G,
-    hid_sem, load_sem, ag_recv, ag_send, kv_recv, kv_send, dk_recv, dk_send,
+    load_sem, ag_recv, ag_send, kv_recv, kv_send, dk_recv, dk_send,
     sib_recv, sib_send, x_recv, x_send, z_recv, z_send,
 ):
     dp = lax.axis_index("dp")
@@ -98,11 +100,26 @@
         )
 
     mine = z * NY + y
-    load_q0 = pltpu.make_async_copy(wq_ref.at[:, pl.ds(0, 128)], W.at[mine, pl.ds(0, 256)], load_sem.at[0])
-    load_q1 = pltpu.make_async_copy(wq_ref.at[:, pl.ds(128, 128)], W.at[mine, pl.ds(256, 256)], load_sem.at[1])
-    load_hid = pltpu.make_async_copy(hid_ref, hid, hid_sem)
-    load_q0.start()
-    load_q1.start()
+
+    def load(k, src, dst):
+        return pltpu.make_async_copy(src, dst, load_sem.at[k])
+
+    load_weights = [
+        load(0, wq_hbm.at[:, pl.ds(0, 128)], W.at[mine, pl.ds(0, 256)]),
+        load(1, wq_hbm.at[:, pl.ds(128, 128)], W.at[mine, pl.ds(256, 256)]),
+        load(2, wk_hbm, wkv.at[0]),
+        load(3, wv_hbm, wkv.at[1]),
+    ]
+    load_rows = [load(4, hid_hbm, hid), load(5, gain_hbm, gain)]
+    load_rest = [
+        load(6, gc_hbm, gc),
+        load(7, cos_hbm, cosine),
+        load(8, sin_hbm, sine),
+        load(9, kcos_hbm.at[rank], kcos),
+        load(10, ksin_hbm.at[rank], ksin),
+    ]
+    for copy in load_weights:
+        copy.start()
     barrier = pltpu.get_barrier_semaphore()
 
     def greet(device):
@@ -119,20 +136,21 @@
     def _():
         greet(down)
 
-    load_hid.start()
-    wk, wv = wk_ref[...].astype(F32), wv_ref[...].astype(F32)
-    packed = jnp.concatenate([wk[:128], wv[:128], wk[128:], wv[128:]], axis=1)
-    W[mine, 512:640, :] = packed.astype(BF16)
-    load_q0.wait()
-    load_q1.wait()
+    for copy in load_rows + load_rest:
+        copy.start()
+    for copy in load_weights:
+        copy.wait()
+    wk, wv = wkv[0].astype(F32), wkv[1].astype(F32)
+    packed = jnp.concatenate([wk[:, :128], wv[:, :128], wk[:, 128:], wv[:, 128:]], axis=0)
+    W[mine, 512:640, :] = packed.T.astype(BF16)
     pl.semaphore_wait(barrier, 7 + jnp.where(z < NZ - 1, 1, 0) + jnp.where(z > 0, 1, 0))
 
-    def block(i, device, kind):
-        return remote(W.at[i], W.at[i], ag_send.at[kind, i], ag_recv.at[i, 0], device)
-
-    def half_block(i, part, device):
-        rows = pl.ds(part * HALF, HALF)
-        return remote(W.at[i, rows], W.at[i, rows], ag_send.at[3, i], ag_recv.at[i, part], device)
+    def block(i, p, device, kind):
+        rows = pl.ds(p * PART, PART)
+        return remote(W.at[i, rows], W.at[i, rows], ag_send.at[kind, i], ag_recv.at[i, p], device)
+
+    def sent(i, rows, device, kind):
+        return remote(W.at[i, rows], W.at[i, rows], ag_send.at[kind, i], ag_recv.at[i, 0], device)
 
     def plane(n):
         s = (n + 1) // 2
@@ -147,19 +165,19 @@
     def go_down(j):
         return jnp.logical_and(j >= z, z > 0)
 
-    def spread(j):
+    def spread(j, p):
         i = j * NY + y
 
         @pl.when(go_up(j))
         def _():
-            block(i, up, 0).start()
+            block(i, p, up, 0).start()
 
         @pl.when(go_down(j))
         def _():
-            block(i, down, 4).start()
-
-        block(i, to_yr, 1).start()
-        block(i, to_yl, 2).start()
+            block(i, p, down, 4).start()
+
+        block(i, p, to_yr, 1).start()
+        block(i, p, to_yl, 2).start()
 
     def multiply(i):
         columns = pl.ds(pl.multiple_of(i * 256, 256), 256)
@@ -170,16 +188,18 @@
         kvacc[0] += dot(rows[:, 0:128], both)
         kvacc[1] += dot(rows[:, 128:256], both)
 
-    spread(z)
+    for p in range(PARTS):
+        spread(z, p)
     qacc[...] = jnp.zeros_like(qacc)
     kvacc[...] = jnp.zeros_like(kvacc)
-    load_hid.wait()
+    for copy in load_rows:
+        copy.wait()
 
     def norm_rows(b, carry):
         rows = pl.ds(pl.multiple_of(b * 16, 16), 16)
         values = hid[rows, :].astype(F32)
         inverse = lax.rsqrt(jnp.mean(values * values, axis=1, keepdims=True) + 1e-05)
-        N[rows, :] = (values * inverse * gain_ref[...]).astype(BF16)
+        N[rows, :] = (values * inverse * gain[...]).astype(BF16)
         return carry
 
     lax.fori_loop(0, SEQ // 16, norm_rows, 0)
@@ -190,40 +210,65 @@
         @pl.when(jnp.logical_and(inside(ja), jnp.logical_and(n > 0, n < 15)))
         def _():
             i = ja * NY + y
-            block(i, up, 0).wait_recv()
-            spread(ja)
-
-        jb = plane(n - 2)
-
-        @pl.when(jnp.logical_and(inside(jb), jnp.logical_and(n >= 2, n < 17)))
+            for p in range(PARTS):
+                block(i, p, up, 0).wait_recv()
+                spread(ja, p)
+
+        jb = plane(n - LAG_B)
+
+        @pl.when(jnp.logical_and(inside(jb), jnp.logical_and(n >= LAG_B, n < 15 + LAG_B)))
         def _():
             i_left, i_right = jb * NY + yl, jb * NY + yr
-            block(i_left, to_yr, 1).wait_recv()
-            half_block(i_left, 0, to_yr).start()
-            block(i_right, to_yl, 2).wait_recv()
-            half_block(i_right, 1, to_yl).start()
+            for p in range(PARTS):
+                block(i_left, p, to_yr, 1).wait_recv()
+                if p < PARTS // 2:
+                    block(i_left, p, to_yr, 3).start()
+                block(i_right, p, to_yl, 2).wait_recv()
+                if p >= PARTS // 2:
+                    block(i_right, p, to_yl, 3).start()
             multiply(jb * NY + y)
             multiply(i_left)
             multiply(i_right)
 
-        jc = plane(n - 4)
-
-        @pl.when(jnp.logical_and(inside(jc), n >= 4))
+        jc = plane(n - LAG_C)
+
+        @pl.when(jnp.logical_and(inside(jc), n >= LAG_C))
         def _():
             i = jc * NY + yo
-            half_block(i, 0, to_yr).wait_recv()
-            half_block(i, 1, to_yl).wait_recv()
+            for p in range(PARTS):
+                block(i, p, to_yr, 3).wait_recv()
             multiply(i)
 
         return carry
 
-    lax.fori_loop(0, 19, gather_step, 0)
+    lax.fori_loop(0, 15 + LAG_C, gather_step, 0)
+
+    for copy in load_rest:
+        copy.wait()
+
+    def gather_sent(j, carry):
+        i = j * NY + y
+        whole = pl.ds(0, ROWS)
+
+        @pl.when(go_up(j))
+        def _():
+            sent(i, whole, up, 0).wait_send()
+
+        @pl.when(go_down(j))
+        def _():
+            sent(i, whole, down, 4).wait_send()
+
+        sent(i, whole, to_yr, 1).wait_send()
+        sent(i, whole, to_yl, 2).wait_send()
+        sent(j * NY + yl, pl.ds(0, ROWS // 2), to_yr, 3).wait_send()
+        sent(j * NY + yr, pl.ds(ROWS // 2, ROWS // 2), to_yl, 3).wait_send()
+        return carry
 
     lane = lax.broadcasted_iota(jnp.int32, (128, 128), 1)
     kva, kvb = kvacc[0], kvacc[1]
     low = kva[:128] + pltpu.roll(kvb[:128], 64, 1)
     high = pltpu.roll(kva[128:], 64, 1) + kvb[128:]
-    kv_own = rotate(jnp.where(lane < 64, low, high), kcos_ref[rank], ksin_ref[rank])
+    kv_own = rotate(jnp.where(lane < 64, low, high), kcos[...], ksin[...])
     kvs[rank] = kv_own.astype(BF16)
 
     def peer(step):
@@ -240,7 +285,7 @@
         kv_copy(step).start()
     q_heads = []
     for h in range(2):
-        q_heads.append(rotate(qacc[h], cos_ref[...], sin_ref[...]).astype(BF16))
+        q_heads.append(rotate(qacc[h], cosine[...], sine[...]).astype(BF16))
     for step in (1, 2, 3):
         kv_copy(step).wait()
 
@@ -264,7 +309,7 @@
     dv = jnp.zeros((SEQ, HD), F32)
     dq_heads = []
     for h in range(2):
-        g_head = gc_ref[:, h * HD : (h + 1) * HD]
+        g_head = gc[:, h * HD : (h + 1) * HD]
         scores = jnp.where(causal, dot_rows(q_heads[h], k_head) * SCALE, -1e30)
         weights = jnp.exp(scores - jnp.max(scores, axis=1, keepdims=True))
         probs = weights / jnp.sum(weights, axis=1, keepdims=True)
@@ -272,7 +317,7 @@
         delta = jnp.sum(probs * grad_probs, axis=1, keepdims=True)
         grad_scores = (probs * (grad_probs - delta) * SCALE).astype(BF16)
         dq = dot(grad_scores, k_head)
-        dq_heads.append(rotate(dq, cos_ref[...], -sin_ref[...]).astype(BF16))
+        dq_heads.append(rotate(dq, cosine[...], -sine[...]).astype(BF16))
         dk = dk + dot_columns(grad_scores, q_heads[h])
         dv = dv + dot_columns(probs.astype(BF16), g_head)
 
@@ -314,7 +359,7 @@
     for step in (1, 2, 3):
         dk_copy(step).wait()
     dkv = dks[rank] + dkr[3].astype(F32) + dkr[4].astype(F32) + dkr[5].astype(F32)
-    dkv = rotate(dkv, kcos_ref[rank], -ksin_ref[rank])
+    dkv = rotate(dkv, kcos[...], -ksin[...])
     turned = pltpu.roll(dkv, 64, 1)
     place(jnp.concatenate([jnp.where(lane < 64, dkv, 0.0), jnp.where(lane < 64, turned, 0.0)], axis=0).astype(BF16), 2)
     place(jnp.concatenate([jnp.where(lane < 64, 0.0, turned), jnp.where(lane < 64, 0.0, dkv)], axis=0).astype(BF16), 3)
@@ -398,7 +443,7 @@
         far_copy(m).wait_recv()
         for h in range(2):
             columns = columns_of(m, h)
-            scaled = (fs[m, zh, h] + zin[m, h].astype(F32)) * gain_ref[:, columns]
+            scaled = (fs[m, zh, h] + zin[m, h].astype(F32)) * gain[:, columns]
             G[m, h] = scaled
             dots = dots + scaled * hid[own_rows, columns].astype(F32)
         return dots
@@ -434,23 +479,6 @@
             value = inverse * (G[m, h] - own_hidden[:, columns] * factor)
             out_ref[:, columns] = value.astype(BF16)
 
-    def gather_sent(j, carry):
-        i = j * NY + y
-
-        @pl.when(go_up(j))
-        def _():
-            block(i, up, 0).wait_send()
-
-        @pl.when(go_down(j))
-        def _():
-            block(i, down, 4).wait_send()
-
-        block(i, to_yr, 1).wait_send()
-        block(i, to_yl, 2).wait_send()
-        half_block(j * NY + yl, 0, to_yr).wait_send()
-        half_block(j * NY + yr, 1, to_yl).wait_send()
-        return carry
-
     lax.fori_loop(0, NZ, gather_sent, 0)
 
     def sum_sent(m, carry):
@@ -469,10 +497,17 @@
     return pl.pallas_call(
         kernel,
         out_shape=jax.ShapeDtypeStruct((16, D), BF16),
-        in_specs=[hbm, vmem, hbm, vmem, vmem, vmem, vmem, vmem, vmem, vmem],
+        in_specs=[hbm] * 10,
         out_specs=vmem,
         scratch_shapes=[
             pltpu.VMEM((SEQ, D), BF16),
+            pltpu.VMEM((1, D), F32),
+            pltpu.VMEM((2, 32, 256), BF16),
+            pltpu.VMEM((SEQ, 256), BF16),
+            pltpu.VMEM((SEQ, HD), F32),
+            pltpu.VMEM((SEQ, HD), F32),
+            pltpu.VMEM((128, 128), F32),
+            pltpu.VMEM((128, 128), F32),
             pltpu.VMEM((SLOTS, ROWS, 128), BF16),
             pltpu.VMEM((SEQ, D), BF16),
             pltpu.VMEM((2, SEQ, HD), F32),
@@ -491,9 +526,8 @@
             pltpu.VMEM((NZ, 2, 16, 512), BF16),
             pltpu.VMEM((NZ, 2, 16, 512), BF16),
             pltpu.VMEM((NZ, 2, 16, 512), F32),
-            dma,
-            dma((2,)),
-            dma((SLOTS, 2)),
+            dma((11,)),
+            dma((SLOTS, PARTS)),
             dma((5, SLOTS)),
             dma((3,)),
             dma((3,)),
@@ -507,10 +541,10 @@
             dma((NZ,)),
         ],
         compiler_params=pltpu.CompilerParams(
-            collective_id=0, has_side_effects=True, vmem_limit_bytes=48 * 1024 * 1024
+            collective_id=0, has_side_effects=True, vmem_limit_bytes=60 * 1024 * 1024
         ),
         name="attention_input_grad",
-    )(hidden, norm_gain.reshape(1, D), w_query, w_key, w_value, grad_context, *tables)
+    )(hidden, norm_gain.reshape(1, D), w_query, w_key.T, w_value.T, grad_context, *tables)
 
 
 def solution(mesh):

time: 126 us -> 110 us (0.87)
  local copies, waits for them, and re-layouts: 10.8 us -> 1.67 us
  Pallas kernels: 115 us -> 108 us
    unnamed x19 -> x1, local copies, waits for them, and re-layouts: 10.8 us -> 1.67 us
    pallas_call x1, Pallas kernels: 115 us -> 108 us  [per_device(): pl.pallas_call(kernel, out_shape=jax.ShapeDtypeStruct((16, D), BF16), in_...]
where the time goes in v2:
time: 110 us
  Pallas kernels  108 us (98%)
  local copies, waits for them, and re-layouts  1.67 us (2%)
    pallas_call x1, Pallas kernels, per_device(): pl.pallas_call(kernel, out_shape=jax.ShapeDtypeStruct((16, D), BF16), in_...  108 us

profile of v2, /device:TPU:1, one launch (start us, length us, event | category | flops | bytes accessed | tf_op | source)
XLA Modules:
  0.0 110.2 jit_solution(13730437709358241480)
XLA Ops:
  0.0 108.5 %attention_input_grad.1 = bf16[16,8192]{1,0:T(8,128)(2,1)} custom-call(bf16[256,8192]{1,0:T(8,128)(2,1)} %hid_hbm.1, f32[1,8192]{1,0:T(1,128)} %bitcast.3, bf16[256,256]{1,0:T(8,128)(2,1)} %wq_hbm.1, bf16[32,256]{1,0:T(8,128)(2,1)} %bitcast.4, bf16[32,256]{1,0:T(8,128)(2,1)} %bitcast.5, bf16[256,256]{1,0:T(8,128)(2,1)} %gc_hbm.1, ...), custom_call_target="tpu_custom_call" | custom-call | tf_op jit(solution)/shard_map/attention_input_grad/pallas_call | solution.py:497
  108.5 1.7 %copy.12 = bf16[16,8192]{1,0:T(8,128)(2,1)} copy(bf16[16,8192]{1,0:T(8,128)(2,1)} %attention_input_grad.1) | data formatting | bytes 524288

commit v3 on v2

v3 whole, which is shorter than its diff:
```python
import functools
import math

import jax
import jax.numpy as jnp
import numpy as np
from jax import lax
from jax.experimental import pallas as pl
from jax.experimental.pallas import tpu as pltpu
from jax.sharding import PartitionSpec as P

D = 8192
HD = 128
SEQ = 256
NZ, NY, NX = 8, 4, 4
PLANES = NZ // 2
SLOTS = PLANES * NY
ROWS = 640
PARTS = 4
PART = ROWS // PARTS
LAG_B, LAG_C = 2, 4
PAIR_STEP, SPREAD_STEP, PARTNER_STEP, PARTNER_PLANES = 4, 8, 9, 4
CHUNKS = 8
LAG_X, LAG_O = 2, 3
ROPE_THETA = 500000.0
SCALE = 1.0 / math.sqrt(HD)
MESH = pl.DeviceIdType.MESH
F32, BF16 = jnp.float32, jnp.bfloat16


def rotary_tables():
    lane = np.arange(HD)
    frequency = np.exp((lane // 2) * (-2.0 * math.log(ROPE_THETA) / HD))
    angle = np.arange(SEQ)[:, None] * frequency[None, :]
    cosine = np.cos(angle)
    sine = np.sin(angle) * np.where(lane % 2 == 0, -1.0, 1.0)[None, :]
    packed_cos = np.ones((4, 128, 128))
    packed_sin = np.zeros((4, 128, 128))
    for rank in range(4):
        columns = slice(32 * rank, 32 * rank + 32)
        for part in range(2):
            rows = slice(128 * part, 128 * part + 128)
            packed_cos[rank, :, 64 * part : 64 * part + 32] = cosine[rows, columns]
            packed_sin[rank, :, 64 * part : 64 * part + 32] = sine[rows, columns]
    return [table.astype(np.float32) for table in (cosine, sine, packed_cos, packed_sin)]


def dot(left, right):
    return lax.dot_general(left, right, (((1,), (0,)), ((), ())), preferred_element_type=F32)


def dot_rows(left, right):
    return lax.dot_general(left, right, (((1,), (1,)), ((), ())), preferred_element_type=F32)


def dot_columns(left, right):
    return lax.dot_general(left, right, (((0,), (0,)), ((), ())), preferred_element_type=F32)


def lanes_of(value):
    return lax.broadcasted_iota(jnp.int32, value.shape, 1)


def rotate(value, cosine, sine):
    left = pltpu.roll(value, 127, 1)
    right = pltpu.roll(value, 1, 1)
    swapped = jnp.where(lanes_of(value) % 2 == 0, left, right)
    return value * cosine + swapped * sine


def kernel(
    hid_hbm, gain_hbm, wq_hbm, wk_hbm, wv_hbm, gc_hbm, cos_hbm, sin_hbm, kcos_hbm, ksin_hbm,
    out_ref,
    hid, gain, wkv, gc, cosine, sine, kcos, ksin, W, N, given, qacc, kvacc, qs, qr, ks, kr,
    kvs, dks, dkr, AQ, AK, dkvs, T, sibs, sibr, own, S, xin, fs, zsend, zin, ps, pr, G, dots,
    load_sem, ag_recv, ag_send, ag_sent, n_recv, n_sent, q_recv, q_send, kv_recv, kv_send, dk_recv, dk_send,
    a_recv, a_send, sib_recv, sib_send, x_recv, x_send, z_recv, z_send, p_recv, p_send,
):
    dp = lax.axis_index("dp")
    tensor = lax.axis_index("tensor")
    z, y = dp // NY, dp % NY
    side, zz = z % 2, z // 2
    zh, x, c = tensor // 8, (tensor // 2) % NX, tensor % 2
    rank = tensor % 4
    share = tensor % 8
    yl, yr, yo = (y + 3) % 4, (y + 1) % 4, (y + 2) % 4
    xl, xr, xo = (x + 3) % 4, (x + 1) % 4, (x + 2) % 4

    def at_dp(zz, yy):
        return (zz * NY + yy, tensor)

    def at_tensor(zhh, xx, cc):
        return (dp, zhh * 8 + xx * 2 + cc)

    up, down = at_dp(z + 2, y), at_dp(z - 2, y)
    pair = at_dp(z + 1 - 2 * side, y)
    to_yl, to_yr = at_dp(z, yl), at_dp(z, yr)
    to_xl, to_xr, to_xo = at_tensor(zh, xl, c), at_tensor(zh, xr, c), at_tensor(zh, xo, c)
    sibling = at_tensor(zh, x, 1 - c)
    far = at_tensor(1 - zh, x, c)
    x_pair = x + 1 - 2 * (x % 2)
    group = {1: sibling, 2: at_tensor(zh, x_pair, c), 3: at_tensor(zh, x_pair, 1 - c)}

    def remote(src, dst, send, recv, device):
        return pltpu.make_async_remote_copy(
            src_ref=src, dst_ref=dst, send_sem=send, recv_sem=recv, device_id=device, device_id_type=MESH
        )

    def plane_start(j, which):
        return (2 * j + which) * 1024

    mine = zz * NY + y

    def load(k, src, dst):
        return pltpu.make_async_copy(src, dst, load_sem.at[k])

    load_weights = [
        load(0, wq_hbm.at[:, pl.ds(0, 128)], W.at[mine, pl.ds(0, 256)]),
        load(1, wq_hbm.at[:, pl.ds(128, 128)], W.at[mine, pl.ds(256, 256)]),
        load(2, wk_hbm, wkv.at[0]),
        load(3, wv_hbm, wkv.at[1]),
    ]
    load_rows = [load(4, hid_hbm, hid), load(5, gain_hbm, gain)]
    load_rest = [
        load(6, gc_hbm, gc),
        load(7, cos_hbm, cosine),
        load(8, sin_hbm, sine),
        load(9, kcos_hbm.at[rank], kcos),
        load(10, ksin_hbm.at[rank], ksin),
    ]
    for copy in load_weights:
        copy.start()
    barrier = pltpu.get_barrier_semaphore()

    def greet(device):
        pl.semaphore_signal(barrier, inc=1, device_id=device, device_id_type=MESH)

    for device in (to_yl, to_yr, to_xl, to_xr, to_xo, sibling, group[3], far, pair):
        greet(device)

    @pl.when(zz < PLANES - 1)
    def _():
        greet(up)

    @pl.when(zz > 0)
    def _():
        greet(down)

    for copy in load_rows + load_rest:
        copy.start()
    for copy in load_weights:
        copy.wait()
    wk, wv = wkv[0].astype(F32), wkv[1].astype(F32)
    packed = jnp.concatenate([wk[:, :128], wv[:, :128], wk[:, 128:], wv[:, 128:]], axis=0)
    W[mine, 512:640, :] = packed.T.astype(BF16)
    pl.semaphore_wait(barrier, 9 + jnp.where(zz < PLANES - 1, 1, 0) + jnp.where(zz > 0, 1, 0))

    def block(i, p, device, kind):
        rows = pl.ds(p * PART, PART)
        if kind in (0, 4):
            send = ag_send.at[kind // 4, i]
        elif kind == 3:
            send = ag_sent.at[2 + p // (PARTS // 2)]
        else:
            send = ag_sent.at[kind - 1]
        return remote(W.at[i, rows], W.at[i, rows], send, ag_recv.at[i, p], device)

    def sent(src, send, device):
        return remote(src, src, send, ag_recv.at[0, 0], device)

    def plane(n):
        s = (n + 1) // 2
        return jnp.where(n % 2 == 1, zz - s, zz + s)

    def inside(j):
        return jnp.logical_and(j >= 0, j < PLANES)

    def go_up(j):
        return jnp.logical_and(j <= zz, zz < PLANES - 1)

    def go_down(j):
        return jnp.logical_and(j >= zz, zz > 0)

    def spread(j, p):
        i = j * NY + y

        @pl.when(go_up(j))
        def _():
            block(i, p, up, 0).start()

        @pl.when(go_down(j))
        def _():
            block(i, p, down, 4).start()

        block(i, p, to_yr, 1).start()
        block(i, p, to_yl, 2).start()

    def rows_of(which, i):
        return N[which, i // 2, :, pl.ds(pl.multiple_of((i % 2) * 256, 256), 256)]

    def multiply_q(which, i):
        rows = rows_of(which, i)
        qacc[which, 0] += dot(rows, W[i, 0:256, :])
        qacc[which, 1] += dot(rows, W[i, 256:512, :])

    def multiply_kv(which, i):
        rows = rows_of(which, i)
        both = W[i, 512:640, :]
        kvacc[which, 0] += dot(rows[:, 0:128], both)
        kvacc[which, 1] += dot(rows[:, 128:256], both)

    def multiply(i):
        multiply_q(0, i)
        multiply_kv(0, i)

    for p in range(PARTS):
        spread(zz, p)
    qacc[...] = jnp.zeros_like(qacc)
    kvacc[...] = jnp.zeros_like(kvacc)

    given_start = pl.multiple_of(plane_start(share // 2, 1 - side) + (share % 2) * 512, 512)

    def norm_rows(b):
        rows = pl.ds(pl.multiple_of(b * 16, 16), 16)
        values = hid[rows, :].astype(F32)
        inverse = lax.rsqrt(jnp.mean(values * values, axis=1, keepdims=True) + 1e-05)

        def normed(start):
            columns = pl.ds(start, 512)
            return (hid[rows, columns].astype(F32) * inverse * gain[:, columns]).astype(BF16)

        given[rows, :] = normed(given_start)
        for e in range(8):
            start = pl.multiple_of(plane_start(e // 2, side) + (e % 2) * 512, 512)
            N[0, e, rows, :] = normed(start)

    def quarter(r):
        return pl.ds(pl.multiple_of(r * 64, 64), 64)

    def give(r):
        return remote(given.at[quarter(r)], N.at[1, share, quarter(r)], n_sent.at[0], n_recv.at[share, r], pair)

    def hand(kind, e, r, device):
        ref = N.at[1, e, quarter(r)]
        return remote(ref, ref, n_sent.at[kind], n_recv.at[e, r], device)

    for copy in load_rows:
        copy.wait()

    def norm_step(r, carry):
        def inner(b, inside_carry):
            norm_rows(r * 4 + b)
            return inside_carry

        lax.fori_loop(0, 4, inner, 0)
        give(r).start()
        return carry

    lax.fori_loop(0, 4, norm_step, 0)

    def spread_given(r, carry):
        give(r).wait_recv()
        hand(1, share, r, to_xr).start()
        hand(2, share, r, to_xl).start()
        hand(3, share, r, to_xo).start()
        hand(4, share, r, sibling).start()
        return carry

    def pass_given(r, carry):
        for xx, device in ((xl, to_xr), (xr, to_xl), (xo, to_xo)):
            e = xx * 2 + c
            hand(1, e, r, device).wait_recv()
            hand(4, e, r, sibling).start()
        return carry

    def wait_given(r, carry):
        for xx in range(NX):
            hand(4, xx * 2 + 1 - c, r, sibling).wait_recv()
        return carry

    def partner_planes(product, first, last):
        def step(n, carry):
            j = plane(n)

            @pl.when(inside(j))
            def _():
                for k in range(NY):
                    product(1, j * NY + k)

            return carry

        lax.fori_loop(first, last, step, 0)

    def gather_step(n, carry):
        @pl.when(n == PAIR_STEP)
        def _():
            lax.fori_loop(0, 4, spread_given, 0)

        @pl.when(n == SPREAD_STEP)
        def _():
            lax.fori_loop(0, 4, pass_given, 0)

        ja = plane(n)

        @pl.when(jnp.logical_and(inside(ja), n < 2 * PLANES - 1))
        def _():
            i = ja * NY + y
            for p in range(PARTS):
                block(i, p, up, 0).wait_recv()
                spread(ja, p)

        jb = plane(n - LAG_B)

        @pl.when(jnp.logical_and(inside(jb), jnp.logical_and(n >= LAG_B, n < 2 * PLANES - 1 + LAG_B)))
        def _():
            i_left, i_right = jb * NY + yl, jb * NY + yr
            for p in range(PARTS):
                block(i_left, p, to_yr, 1).wait_recv()
                if p < PARTS // 2:
                    block(i_left, p, to_yr, 3).start()
                block(i_right, p, to_yl, 2).wait_recv()
                if p >= PARTS // 2:
                    block(i_right, p, to_yl, 3).start()
            multiply(jb * NY + y)
            multiply(i_left)
            multiply(i_right)

        jc = plane(n - LAG_C)

        @pl.when(jnp.logical_and(inside(jc), n >= LAG_C))
        def _():
            i = jc * NY + yo
            for p in range(PARTS):
                block(i, p, to_yr, 3).wait_recv()
            multiply(i)

        @pl.when(n == PARTNER_STEP)
        def _():
            lax.fori_loop(0, 4, wait_given, 0)
            partner_planes(multiply_q, 0, PARTNER_PLANES)
            partner_planes(multiply_kv, 0, PARTNER_PLANES)

        return carry

    lax.fori_loop(1, 2 * PLANES - 1 + LAG_C, gather_step, 0)

    for copy in load_rest:
        copy.wait()

    def gather_sent():
        def chain_sent(j, carry):
            i = j * NY + y

            @pl.when(go_up(j))
            def _():
                sent(W.at[i], ag_send.at[0, i], up).wait_send()

            @pl.when(go_down(j))
            def _():
                sent(W.at[i], ag_send.at[1, i], down).wait_send()

            return carry

        lax.fori_loop(0, PLANES, chain_sent, 0)
        all_blocks, all_halves = W.at[pl.ds(0, PLANES)], W.at[pl.ds(0, PLANES), pl.ds(0, ROWS // 2)]
        sent(all_blocks, ag_sent.at[0], to_yr).wait_send()
        sent(all_blocks, ag_sent.at[1], to_yl).wait_send()
        sent(all_halves, ag_sent.at[2], to_yr).wait_send()
        sent(all_halves, ag_sent.at[3], to_yl).wait_send()
        sent(given, n_sent.at[0], pair).wait_send()
        for kind, device in ((1, to_xr), (2, to_xl), (3, to_xo)):
            sent(given, n_sent.at[kind], device).wait_send()
        sent(N.at[1, pl.ds(0, 4)], n_sent.at[4], sibling).wait_send()

    lane = lax.broadcasted_iota(jnp.int32, (128, 128), 1)

    def pack_kv(which):
        kva, kvb = kvacc[which, 0], kvacc[which, 1]
        low = kva[:128] + pltpu.roll(kvb[:128], 64, 1)
        high = pltpu.roll(kva[128:], 64, 1) + kvb[128:]
        return jnp.where(lane < 64, low, high)

    def ks_copy():
        return remote(ks, kr, q_send.at[0], q_recv.at[0], pair)

    def qs_copy(h):
        return remote(qs.at[h], qr.at[h], q_send.at[1 + h], q_recv.at[1 + h], pair)

    partner_planes(multiply_kv, PARTNER_PLANES, 2 * PLANES - 1)
    ks[...] = pack_kv(1).astype(BF16)
    ks_copy().start()
    partner_planes(multiply_q, PARTNER_PLANES, 2 * PLANES - 1)
    for h in range(2):
        qs[h] = qacc[1, h].astype(BF16)
        qs_copy(h).start()

    kv_mine = pack_kv(0)
    gather_sent()
    ks_copy().wait()
    kv_own = rotate(kv_mine + kr[...].astype(F32), kcos[...], ksin[...])
    kvs[rank] = kv_own.astype(BF16)

    def peer(step):
        if step == 1:
            return rank + 1 - 2 * (rank % 2)
        if step == 2:
            return (rank + 2) % 4
        return 3 - rank

    def kv_copy(step):
        return remote(kvs.at[rank], kvs.at[rank], kv_send.at[step - 1], kv_recv.at[step - 1], group[step])

    for step in (1, 2, 3):
        kv_copy(step).start()
    q_heads = []
    for h in range(2):
        qs_copy(h).wait()
        q_sum = qacc[0, h] + qr[h].astype(F32)
        q_heads.append(rotate(q_sum, cosine[...], sine[...]).astype(BF16))
    for step in (1, 2, 3):
        kv_copy(step).wait()

    def unpack(shift):
        parts = []
        for part in range(2):
            total = jnp.zeros((128, 128), F32)
            for r in range(4):
                piece = kvs[r].astype(F32)
                amount = (32 * r - shift - 64 * part) % 128
                piece = pltpu.roll(piece, amount, 1) if amount else piece
                total = jnp.where(lane // 32 == r, piece, total)
            parts.append(total)
        return jnp.concatenate(parts, axis=0).astype(BF16)

    k_head, v_head = unpack(0), unpack(32)
    row_id = lax.broadcasted_iota(jnp.int32, (SEQ, SEQ), 0)
    col_id = lax.broadcasted_iota(jnp.int32, (SEQ, SEQ), 1)
    causal = row_id >= col_id
    dk = jnp.zeros((SEQ, HD), F32)
    dv = jnp.zeros((SEQ, HD), F32)
    dq_heads = []
    for h in range(2):
        g_head = gc[:, h * HD : (h + 1) * HD]
        scores = jnp.where(causal, dot_rows(q_heads[h], k_head) * SCALE, -1e30)
        weights = jnp.exp(scores - jnp.max(scores, axis=1, keepdims=True))
        probs = weights / jnp.sum(weights, axis=1, keepdims=True)
        grad_probs = dot_rows(g_head, v_head)
        delta = jnp.sum(probs * grad_probs, axis=1, keepdims=True)
        grad_scores = (probs * (grad_probs - delta) * SCALE).astype(BF16)
        dq = dot(grad_scores, k_head)
        dq_heads.append(rotate(dq, cosine[...], -sine[...]).astype(BF16))
        dk = dk + dot_columns(grad_scores, q_heads[h])
        dv = dv + dot_columns(probs.astype(BF16), g_head)

    def pack(r):
        def shifted(value, amount):
            amount = amount % 128
            return pltpu.roll(value, amount, 1) if amount else value

        total = shifted(dk[:128], -32 * r)
        total = jnp.where(lane // 32 == 1, shifted(dv[:128], 32 - 32 * r), total)
        total = jnp.where(lane // 32 == 2, shifted(dk[128:], 64 - 32 * r), total)
        return jnp.where(lane // 32 == 3, shifted(dv[128:], 96 - 32 * r), total)

    for r in range(4):
        dks[r] = pack(r)
    for step in (1, 2, 3):
        dkr[step - 1] = dks[peer(step)].astype(BF16)

    def dk_copy(step):
        return remote(dkr.at[step - 1], dkr.at[step + 2], dk_send.at[step - 1], dk_recv.at[step - 1], group[step])

    for step in (1, 2, 3):
        dk_copy(step).start()

    def ordered(value, core):
        return jnp.concatenate(
            [value[16 * (8 * b + 2 * a + core) : 16 * (8 * b + 2 * a + core) + 16] for a in range(NX) for b in range(2)],
            axis=0,
        )

    def place(ref, value):
        for core in range(2):
            start = pl.multiple_of(jnp.where(c == core, 128, 0), 128)
            ref[pl.ds(start, 128), :] = ordered(value, core)

    def place_kv(which, value):
        turned = pltpu.roll(value, 64, 1)
        first = jnp.concatenate([jnp.where(lane < 64, value, 0.0), jnp.where(lane < 64, turned, 0.0)], axis=0)
        second = jnp.concatenate([jnp.where(lane < 64, 0.0, turned), jnp.where(lane < 64, 0.0, value)], axis=0)
        place(AK.at[which, 0], first.astype(BF16))
        place(AK.at[which, 1], second.astype(BF16))

    def aq_copy():
        return remote(AQ.at[0], AQ.at[1], a_send.at[0], a_recv.at[0], pair)

    def ak_copy():
        return remote(dkvs.at[0], dkvs.at[1], a_send.at[1], a_recv.at[1], pair)

    place(AQ.at[0], jnp.concatenate(dq_heads, axis=1))
    aq_copy().start()

    def weights_q(i):
        return jnp.concatenate([W[i, 0:256, :], W[i, 256:512, :]], axis=1)

    def query_term(j, carry):
        dq = AQ[0]
        for k in range(NY):
            T[j, k] = dot_rows(dq, weights_q(j * NY + k))
        return carry

    lax.fori_loop(0, PLANES, query_term, 0)
    for step in (1, 2, 3):
        dk_copy(step).wait()
    dkv = dks[rank] + dkr[3].astype(F32) + dkr[4].astype(F32) + dkr[5].astype(F32)
    dkv = rotate(dkv, kcos[...], -ksin[...]).astype(BF16)
    dkvs[0] = dkv
    ak_copy().start()
    place_kv(0, dkv.astype(F32))

    def sib_copy(m):
        return remote(sibs.at[m], sibr.at[m], sib_send.at[0], sib_recv.at[m], sibling)

    def x_copy(kind, m):
        x_dst, h, device = ((xo, 0, to_xr), (xo, 1, to_xl), (xr, 1, to_xr), (xl, 0, to_xl), (xr, 0, to_xr), (xl, 1, to_xl))[kind]
        return remote(S.at[m, x_dst, h], xin.at[m, kind], x_send.at[kind], x_recv.at[m, kind], device)

    def far_copy(m):
        return remote(zsend.at[m], zin.at[m], z_send.at[0], z_recv.at[m], far)

    def chunk(m):
        partner = jnp.logical_and(m >= 2, m < 6)
        return partner, jnp.where(m < 2, m, jnp.where(m < 6, m - 2, m - 4))

    def term(m):
        partner, j = chunk(m)

        def add_term(which):
            dkv_a, dkv_b = AK[which, 0], AK[which, 1]
            for k in range(NY):
                i = j * NY + k
                both = W[i, 512:640, :]
                base = T[j, k] if which == 0 else dot_rows(AQ[1], weights_q(i))
                value = base + jnp.concatenate([dot_rows(dkv_a, both), dot_rows(dkv_b, both)], axis=1)
                columns = slice((k % 2) * 256, (k % 2) * 256 + 256)
                sibs[m, k // 2, :, columns] = value[:128].astype(BF16)
                own[m, k // 2, :, columns] = value[128:]

        @pl.when(jnp.logical_not(partner))
        def _():
            add_term(0)

        @pl.when(partner)
        def _():
            add_term(1)

        sib_copy(m).start()

    def over_cores(m):
        sib_copy(m).wait_recv()
        for h in range(2):
            for a in range(NX):
                rows = slice(32 * a, 32 * a + 32)
                S[m, a, h] = (own[m, h, rows, :] + sibr[m, h, rows, :].astype(F32)).astype(BF16)

        for kind in (0, 1, 2, 3):
            x_copy(kind, m).start()

    def over_x(m):
        x_copy(0, m).wait_recv()
        S[m, xr, 0] = (S[m, xr, 0].astype(F32) + xin[m, 0].astype(F32)).astype(BF16)
        x_copy(4, m).start()
        x_copy(1, m).wait_recv()
        S[m, xl, 1] = (S[m, xl, 1].astype(F32) + xin[m, 1].astype(F32)).astype(BF16)
        x_copy(5, m).start()

    def send_far(m, totals):
        for h in range(2):
            fs[m, 0, h] = totals[h][0:16]
            fs[m, 1, h] = totals[h][16:32]
        zsend[m] = fs[m, 1 - zh].astype(BF16)
        far_copy(m).start()

    def at_owner_x(m):
        for kind in (2, 3, 4, 5):
            x_copy(kind, m).wait_recv()
        totals = [
            S[m, x, 0].astype(F32) + xin[m, 3].astype(F32) + xin[m, 4].astype(F32),
            S[m, x, 1].astype(F32) + xin[m, 2].astype(F32) + xin[m, 5].astype(F32),
        ]
        send_far(m, totals)

    own_rows = pl.ds(pl.multiple_of(tensor * 16, 16), 16)

    def pair_copy(j):
        return remote(ps.at[j], pr.at[j], p_send.at[0], p_recv.at[j], pair)

    def scale_plane(j, which, h, value, dots):
        columns = pl.ds(pl.multiple_of(plane_start(j, which) + h * 512, 512), 512)
        scaled = value * gain[:, columns]
        G[2 * j + which, h] = scaled
        dots[...] += scaled * hid[own_rows, columns].astype(F32)

    def at_owner(m, carry):
        partner, j = chunk(m)
        far_copy(m).wait_recv()

        @pl.when(jnp.logical_not(partner))
        def _():
            for h in range(2):
                scale_plane(j, side, h, fs[m, zh, h] + zin[m, h].astype(F32), dots)

        @pl.when(partner)
        def _():
            ps[j] = (fs[m, zh] + zin[m].astype(F32)).astype(BF16)
            pair_copy(j).start()

        return carry

    def from_partner(j, carry):
        pair_copy(j).wait_recv()
        for h in range(2):
            scale_plane(j, 1 - side, h, pr[j, h].astype(F32), dots)
        return carry

    dots[...] = jnp.zeros_like(dots)

    def sum_step(n, carry):
        @pl.when(n == 2)
        def _():
            aq_copy().wait()
            ak_copy().wait()
            place_kv(1, dkvs[1].astype(F32))

        @pl.when(n < CHUNKS)
        def _():
            term(n)

        @pl.when(jnp.logical_and(n >= 1, n < CHUNKS + 1))
        def _():
            over_cores(n - 1)

        @pl.when(jnp.logical_and(n >= LAG_X, n < CHUNKS + LAG_X))
        def _():
            over_x(n - LAG_X)

        @pl.when(n >= LAG_O)
        def _():
            at_owner_x(n - LAG_O)

        return carry

    lax.fori_loop(0, CHUNKS + LAG_O, sum_step, 0)

    remote(sibs, sibr, sib_send.at[0], sib_recv.at[0], sibling).wait_send()
    for kind in range(6):
        x_dst = (to_xr, to_xl)[kind % 2]
        remote(S.at[:, 0, 0], xin.at[:, 0], x_send.at[kind], x_recv.at[0, 0], x_dst).wait_send()
    lax.fori_loop(0, 6, at_owner, 0)
    lax.fori_loop(0, PLANES, from_partner, 0)
    lax.fori_loop(6, CHUNKS, at_owner, 0)
    mean_term = jnp.sum(dots[...], axis=1, keepdims=True) * (1.0 / D)
    own_hidden = hid[own_rows, :].astype(F32)
    inverse = lax.rsqrt(jnp.mean(own_hidden * own_hidden, axis=1, keepdims=True) + 1e-05)
    factor = inverse * inverse * mean_term
    for m in range(NZ):
        for h in range(2):
            columns = slice(m * 1024 + h * 512, m * 1024 + h * 512 + 512)
            value = inverse * (G[m, h] - own_hidden[:, columns] * factor)
            out_ref[:, columns] = value.astype(BF16)

    remote(zsend, zin, z_send.at[0], z_recv.at[0], far).wait_send()
    remote(ps, pr, p_send.at[0], p_recv.at[0], pair).wait_send()


def per_device(hidden, norm_gain, w_query, w_key, w_value, grad_context):
    tables = [jnp.asarray(table) for table in rotary_tables()]
    vmem = pl.BlockSpec(memory_space=pltpu.VMEM)
    hbm = pl.BlockSpec(memory_space=pl.ANY)
    dma = pltpu.SemaphoreType.DMA
    return pl.pallas_call(
        kernel,
        out_shape=jax.ShapeDtypeStruct((16, D), BF16),
        in_specs=[hbm] * 10,
        out_specs=vmem,
        scratch_shapes=[
            pltpu.VMEM((SEQ, D), BF16),
            pltpu.VMEM((1, D), F32),
            pltpu.VMEM((2, 32, 256), BF16),
            pltpu.VMEM((SEQ, 256), BF16),
            pltpu.VMEM((SEQ, HD), F32),
            pltpu.VMEM((SEQ, HD), F32),
            pltpu.VMEM((128, 128), F32),
            pltpu.VMEM((128, 128), F32),
            pltpu.VMEM((SLOTS, ROWS, 128), BF16),
            pltpu.VMEM((2, 8, SEQ, 512), BF16),
            pltpu.VMEM((SEQ, 512), BF16),
            pltpu.VMEM((2, 2, SEQ, HD), F32),
            pltpu.VMEM((2, 2, SEQ, HD), F32),
            pltpu.VMEM((2, SEQ, HD), BF16),
            pltpu.VMEM((2, SEQ, HD), BF16),
            pltpu.VMEM((128, 128), BF16),
            pltpu.VMEM((128, 128), BF16),
            pltpu.VMEM((4, 128, 128), BF16),
            pltpu.VMEM((4, 128, 128), F32),
            pltpu.VMEM((6, 128, 128), BF16),
            pltpu.VMEM((2, SEQ, 256), BF16),
            pltpu.VMEM((2, 2, SEQ, 128), BF16),
            pltpu.VMEM((2, 128, 128), BF16),
            pltpu.VMEM((PLANES, NY, SEQ, 256), F32),
            pltpu.VMEM((CHUNKS, 2, 128, 512), BF16),
            pltpu.VMEM((CHUNKS, 2, 128, 512), BF16),
            pltpu.VMEM((CHUNKS, 2, 128, 512), F32),
            pltpu.VMEM((CHUNKS, NX, 2, 32, 512), BF16),
            pltpu.VMEM((CHUNKS, 6, 32, 512), BF16),
            pltpu.VMEM((CHUNKS, 2, 2, 16, 512), F32),
            pltpu.VMEM((CHUNKS, 2, 16, 512), BF16),
            pltpu.VMEM((CHUNKS, 2, 16, 512), BF16),
            pltpu.VMEM((PLANES, 2, 16, 512), BF16),
            pltpu.VMEM((PLANES, 2, 16, 512), BF16),
            pltpu.VMEM((NZ, 2, 16, 512), F32),
            pltpu.VMEM((16, 512), F32),
            dma((11,)),
            dma((SLOTS, PARTS)),
            dma((2, SLOTS)),
            dma((4,)),
            dma((8, 4)),
            dma((5,)),
            dma((3,)),
            dma((3,)),
            dma((3,)),
            dma((3,)),
            dma((3,)),
            dma((3,)),
            dma((2,)),
            dma((2,)),
            dma((CHUNKS,)),
            dma((1,)),
            dma((CHUNKS, 6)),
            dma((6,)),
            dma((CHUNKS,)),
            dma((1,)),
            dma((PLANES,)),
            dma((1,)),
        ],
        compiler_params=pltpu.CompilerParams(
            collective_id=0, has_side_effects=True, vmem_limit_bytes=60 * 1024 * 1024
        ),
        name="attention_input_grad",
    )(hidden, norm_gain.reshape(1, D), w_query, w_key.T, w_value.T, grad_context, *tables)


def solution(mesh):
    in_specs = (
        P("dp", None),
        P(),
        P("dp", "tensor"),
        P("dp", "tensor"),
        P("dp", "tensor"),
        P("dp", "tensor"),
    )
    out_specs = P(("dp", "tensor"), None)
    return jax.shard_map(
        per_device, mesh=mesh, in_specs=in_specs, out_specs=out_specs, check_vma=False
    )
```

time: 110 us -> 106 us (0.964)
  Pallas kernels: 108 us -> 104 us
    pallas_call x1, Pallas kernels: 108 us -> 104 us  [per_device(): pl.pallas_call(kernel, out_shape=jax.ShapeDtypeStruct((16, D), BF16), in_...]
where the time goes in v3:
time: 106 us
  Pallas kernels  104 us (98%)
  local copies, waits for them, and re-layouts  1.67 us (2%)
    pallas_call x1, Pallas kernels, per_device(): pl.pallas_call(kernel, out_shape=jax.ShapeDtypeStruct((16, D), BF16), in_...  104 us

profile of v3, /device:TPU:1, one launch (start us, length us, event | category | flops | bytes accessed | tf_op | source)
XLA Modules:
  0.0 105.5 jit_solution(11921816494011076768)
XLA Ops:
  0.0 103.8 %attention_input_grad.1 = bf16[16,8192]{1,0:T(8,128)(2,1)} custom-call(bf16[256,8192]{1,0:T(8,128)(2,1)} %hid_hbm.1, f32[1,8192]{1,0:T(1,128)} %bitcast.3, bf16[256,256]{1,0:T(8,128)(2,1)} %wq_hbm.1, bf16[32,256]{1,0:T(8,128)(2,1)} %bitcast.4, bf16[32,256]{1,0:T(8,128)(2,1)} %bitcast.5, bf16[256,256]{1,0:T(8,128)(2,1)} %gc_hbm.1, ...), custom_call_target="tpu_custom_call" | custom-call | tf_op jit(solution)/shard_map/attention_input_grad/pallas_call | solution.py:681
  103.8 1.7 %copy.12 = bf16[16,8192]{1,0:T(8,128)(2,1)} copy(bf16[16,8192]{1,0:T(8,128)(2,1)} %attention_input_grad.1) | data formatting | bytes 524288

commit v4 on v3

--- a/solution.py
+++ b/solution.py
@@ -20,6 +20,7 @@
 PART = ROWS // PARTS
 LAG_B, LAG_C = 2, 4
 PAIR_STEP, SPREAD_STEP, PARTNER_STEP, PARTNER_PLANES = 4, 8, 9, 4
+WORD_STEPS = (3, 5, 7, 10)
 CHUNKS = 8
 LAG_X, LAG_O = 2, 3
 ROPE_THETA = 500000.0
@@ -73,7 +74,7 @@
     out_ref,
     hid, gain, wkv, gc, cosine, sine, kcos, ksin, W, N, given, qacc, kvacc, qs, qr, ks, kr,
     kvs, dks, dkr, AQ, AK, dkvs, T, sibs, sibr, own, S, xin, fs, zsend, zin, ps, pr, G, dots,
-    load_sem, ag_recv, ag_send, ag_sent, n_recv, n_sent, q_recv, q_send, kv_recv, kv_send, dk_recv, dk_send,
+    word, load_sem, ag_recv, ag_send, ag_sent, n_recv, n_sent, q_recv, q_send, kv_recv, kv_send, dk_recv, dk_send,
     a_recv, a_send, sib_recv, sib_send, x_recv, x_send, z_recv, z_send, p_recv, p_send,
 ):
     dp = lax.axis_index("dp")
@@ -135,16 +136,14 @@
     def greet(device):
         pl.semaphore_signal(barrier, inc=1, device_id=device, device_id_type=MESH)
 
-    for device in (to_yl, to_yr, to_xl, to_xr, to_xo, sibling, group[3], far, pair):
+    def two_planes(step):
+        there = z + step
+        other = jnp.where(jnp.logical_and(there >= 0, there < NZ), zh, 1 - zh)
+        return ((there + NZ) % NZ * NY + y, other * 8 + share)
+
+    ring_up, ring_down = two_planes(2), two_planes(-2)
+    for device in (to_yl, to_yr, to_xl, to_xr, to_xo, sibling, group[3], pair, ring_up, ring_down):
         greet(device)
-
-    @pl.when(zz < PLANES - 1)
-    def _():
-        greet(up)
-
-    @pl.when(zz > 0)
-    def _():
-        greet(down)
 
     for copy in load_rows + load_rest:
         copy.start()
@@ -153,7 +152,12 @@
     wk, wv = wkv[0].astype(F32), wkv[1].astype(F32)
     packed = jnp.concatenate([wk[:, :128], wv[:, :128], wk[:, 128:], wv[:, 128:]], axis=0)
     W[mine, 512:640, :] = packed.T.astype(BF16)
-    pl.semaphore_wait(barrier, 9 + jnp.where(zz < PLANES - 1, 1, 0) + jnp.where(zz > 0, 1, 0))
+    pl.semaphore_wait(barrier, 10)
+
+    def pass_word(k):
+        pl.semaphore_signal(word.at[k], inc=1, device_id=ring_up, device_id_type=MESH)
+
+    pass_word(0)
 
     def block(i, p, device, kind):
         rows = pl.ds(p * PART, PART)
@@ -292,6 +296,14 @@
         lax.fori_loop(first, last, step, 0)
 
     def gather_step(n, carry):
+        for k in range(4):
+
+            @pl.when(n == WORD_STEPS[k])
+            def _(k=k):
+                pl.semaphore_wait(word.at[k], 1)
+                if k < 3:
+                    pass_word(k + 1)
+
         @pl.when(n == PAIR_STEP)
         def _():
             lax.fori_loop(0, 4, spread_given, 0)
@@ -720,6 +732,7 @@
             pltpu.VMEM((PLANES, 2, 16, 512), BF16),
             pltpu.VMEM((NZ, 2, 16, 512), F32),
             pltpu.VMEM((16, 512), F32),
+            pltpu.SemaphoreType.REGULAR((4,)),
             dma((11,)),
             dma((SLOTS, PARTS)),
             dma((2, SLOTS)),

time: 106 us -> 102 us (0.962)
  Pallas kernels: 104 us -> 99.9 us
    pallas_call x1, Pallas kernels: 104 us -> 99.9 us  [per_device(): pl.pallas_call(kernel, out_shape=jax.ShapeDtypeStruct((16, D), BF16), in_...]
where the time goes in v4:
time: 102 us
  Pallas kernels  99.9 us (98%)
  local copies, waits for them, and re-layouts  1.67 us (2%)
    pallas_call x1, Pallas kernels, per_device(): pl.pallas_call(kernel, out_shape=jax.ShapeDtypeStruct((16, D), BF16), in_...  99.9 us

profile of v4, /device:TPU:1, one launch (start us, length us, event | category | flops | bytes accessed | tf_op | source)
XLA Modules:
  0.0 101.6 jit_solution(94442588908153804)
XLA Ops:
  0.0 99.9 %attention_input_grad.1 = bf16[16,8192]{1,0:T(8,128)(2,1)} custom-call(bf16[256,8192]{1,0:T(8,128)(2,1)} %hid_hbm.1, f32[1,8192]{1,0:T(1,128)} %bitcast.3, bf16[256,256]{1,0:T(8,128)(2,1)} %wq_hbm.1, bf16[32,256]{1,0:T(8,128)(2,1)} %bitcast.4, bf16[32,256]{1,0:T(8,128)(2,1)} %bitcast.5, bf16[256,256]{1,0:T(8,128)(2,1)} %gc_hbm.1, ...), custom_call_target="tpu_custom_call" | custom-call | tf_op jit(solution)/shard_map/attention_input_grad/pallas_call | solution.py:693
  99.9 1.7 %copy.12 = bf16[16,8192]{1,0:T(8,128)(2,1)} copy(bf16[16,8192]{1,0:T(8,128)(2,1)} %attention_input_grad.1) | data formatting | bytes 524288

commit v5 on v4

--- a/solution.py
+++ b/solution.py
@@ -19,7 +19,7 @@
 PARTS = 4
 PART = ROWS // PARTS
 LAG_B, LAG_C = 2, 4
-PAIR_STEP, SPREAD_STEP, PARTNER_STEP, PARTNER_PLANES = 4, 8, 9, 4
+PAIR_STEP, SPREAD_STEP, PARTNER_STEP, PARTNER_PLANES = 5, 9, 10, 4
 WORD_STEPS = (3, 5, 7, 10)
 CHUNKS = 8
 LAG_X, LAG_O = 2, 3
@@ -99,6 +99,7 @@
     to_xl, to_xr, to_xo = at_tensor(zh, xl, c), at_tensor(zh, xr, c), at_tensor(zh, xo, c)
     sibling = at_tensor(zh, x, 1 - c)
     far = at_tensor(1 - zh, x, c)
+    far_pair = ((z + 1 - 2 * side) * NY + y, (1 - zh) * 8 + share)
     x_pair = x + 1 - 2 * (x % 2)
     group = {1: sibling, 2: at_tensor(zh, x_pair, c), 3: at_tensor(zh, x_pair, 1 - c)}
 
@@ -257,7 +258,6 @@
             return inside_carry
 
         lax.fori_loop(0, 4, inner, 0)
-        give(r).start()
         return carry
 
     lax.fori_loop(0, 4, norm_step, 0)
@@ -320,6 +320,22 @@
             for p in range(PARTS):
                 block(i, p, up, 0).wait_recv()
                 spread(ja, p)
+
+        @pl.when(n == 2)
+        def _():
+            give(0).start()
+
+        @pl.when(n == 2)
+        def _():
+            give(1).start()
+
+        @pl.when(n == 3)
+        def _():
+            give(2).start()
+
+        @pl.when(n == 3)
+        def _():
+            give(3).start()
 
         jb = plane(n - LAG_B)
 
@@ -537,8 +553,11 @@
         x_dst, h, device = ((xo, 0, to_xr), (xo, 1, to_xl), (xr, 1, to_xr), (xl, 0, to_xl), (xr, 0, to_xr), (xl, 1, to_xl))[kind]
         return remote(S.at[m, x_dst, h], xin.at[m, kind], x_send.at[kind], x_recv.at[m, kind], device)
 
-    def far_copy(m):
-        return remote(zsend.at[m], zin.at[m], z_send.at[0], z_recv.at[m], far)
+    def far_copy(m, device):
+        return remote(zsend.at[m], zin.at[m], z_send.at[0], z_recv.at[m], device)
+
+    def pair_copy(j):
+        return remote(ps.at[j], pr.at[j], p_send.at[0], p_recv.at[j], pair)
 
     def chunk(m):
         partner = jnp.logical_and(m >= 2, m < 6)
@@ -587,11 +606,21 @@
         x_copy(5, m).start()
 
     def send_far(m, totals):
+        partner, j = chunk(m)
         for h in range(2):
             fs[m, 0, h] = totals[h][0:16]
             fs[m, 1, h] = totals[h][16:32]
         zsend[m] = fs[m, 1 - zh].astype(BF16)
-        far_copy(m).start()
+
+        @pl.when(jnp.logical_not(partner))
+        def _():
+            far_copy(m, far).start()
+
+        @pl.when(partner)
+        def _():
+            far_copy(m, far_pair).start()
+            ps[j] = fs[m, zh].astype(BF16)
+            pair_copy(j).start()
 
     def at_owner_x(m):
         for kind in (2, 3, 4, 5):
@@ -604,10 +633,7 @@
 
     own_rows = pl.ds(pl.multiple_of(tensor * 16, 16), 16)
 
-    def pair_copy(j):
-        return remote(ps.at[j], pr.at[j], p_send.at[0], p_recv.at[j], pair)
-
-    def scale_plane(j, which, h, value, dots):
+    def scale_plane(j, which, h, value):
         columns = pl.ds(pl.multiple_of(plane_start(j, which) + h * 512, 512), 512)
         scaled = value * gain[:, columns]
         G[2 * j + which, h] = scaled
@@ -615,24 +641,19 @@
 
     def at_owner(m, carry):
         partner, j = chunk(m)
-        far_copy(m).wait_recv()
+        far_copy(m, far).wait_recv()
 
         @pl.when(jnp.logical_not(partner))
         def _():
             for h in range(2):
-                scale_plane(j, side, h, fs[m, zh, h] + zin[m, h].astype(F32), dots)
+                scale_plane(j, side, h, fs[m, zh, h] + zin[m, h].astype(F32))
 
         @pl.when(partner)
         def _():
-            ps[j] = (fs[m, zh] + zin[m].astype(F32)).astype(BF16)
-            pair_copy(j).start()
-
-        return carry
-
-    def from_partner(j, carry):
-        pair_copy(j).wait_recv()
-        for h in range(2):
-            scale_plane(j, 1 - side, h, pr[j, h].astype(F32), dots)
+            pair_copy(j).wait_recv()
+            for h in range(2):
+                scale_plane(j, 1 - side, h, pr[j, h].astype(F32) + zin[m, h].astype(F32))
+
         return carry
 
     dots[...] = jnp.zeros_like(dots)
@@ -668,9 +689,7 @@
     for kind in range(6):
         x_dst = (to_xr, to_xl)[kind % 2]
         remote(S.at[:, 0, 0], xin.at[:, 0], x_send.at[kind], x_recv.at[0, 0], x_dst).wait_send()
-    lax.fori_loop(0, 6, at_owner, 0)
-    lax.fori_loop(0, PLANES, from_partner, 0)
-    lax.fori_loop(6, CHUNKS, at_owner, 0)
+    lax.fori_loop(0, CHUNKS, at_owner, 0)
     mean_term = jnp.sum(dots[...], axis=1, keepdims=True) * (1.0 / D)
     own_hidden = hid[own_rows, :].astype(F32)
     inverse = lax.rsqrt(jnp.mean(own_hidden * own_hidden, axis=1, keepdims=True) + 1e-05)

time: 102 us -> 99.8 us (0.978)
  Pallas kernels: 99.9 us -> 97.8 us
    pallas_call x1, Pallas kernels: 99.9 us -> 97.8 us  [per_device(): pl.pallas_call(kernel, out_shape=jax.ShapeDtypeStruct((16, D), BF16), in_...]
where the time goes in v5:
time: 99.8 us; the launch traced here: 99.5 us
  Pallas kernels  97.8 us (98%)
  local copies, waits for them, and re-layouts  1.67 us (2%)
    pallas_call x1, Pallas kernels, per_device(): pl.pallas_call(kernel, out_shape=jax.ShapeDtypeStruct((16, D), BF16), in_...  97.8 us

profile of v5, /device:TPU:1, one launch (start us, length us, event | category | flops | bytes accessed | tf_op | source)
XLA Modules:
  0.0 99.5 jit_solution(17461067186531748382)
XLA Ops:
  0.0 97.8 %attention_input_grad.1 = bf16[16,8192]{1,0:T(8,128)(2,1)} custom-call(bf16[256,8192]{1,0:T(8,128)(2,1)} %hid_hbm.1, f32[1,8192]{1,0:T(1,128)} %bitcast.3, bf16[256,256]{1,0:T(8,128)(2,1)} %wq_hbm.1, bf16[32,256]{1,0:T(8,128)(2,1)} %bitcast.4, bf16[32,256]{1,0:T(8,128)(2,1)} %bitcast.5, bf16[256,256]{1,0:T(8,128)(2,1)} %gc_hbm.1, ...), custom_call_target="tpu_custom_call" | custom-call | tf_op jit(solution)/shard_map/attention_input_grad/pallas_call | solution.py:712
  97.8 1.7 %copy.12 = bf16[16,8192]{1,0:T(8,128)(2,1)} copy(bf16[16,8192]{1,0:T(8,128)(2,1)} %attention_input_grad.1) | data formatting | bytes 524288

commit v6 on v5

--- a/solution.py
+++ b/solution.py
@@ -304,9 +304,13 @@
                 if k < 3:
                     pass_word(k + 1)
 
+        @pl.when(n == PAIR_STEP - 1)
+        def _():
+            lax.fori_loop(0, 2, spread_given, 0)
+
         @pl.when(n == PAIR_STEP)
         def _():
-            lax.fori_loop(0, 4, spread_given, 0)
+            lax.fori_loop(2, 4, spread_given, 0)
 
         @pl.when(n == SPREAD_STEP)
         def _():

time: 99.8 us -> 102 us (1.022)
  Pallas kernels: 97.8 us -> 100 us
    pallas_call x1, Pallas kernels: 97.8 us -> 100 us  [per_device(): pl.pallas_call(kernel, out_shape=jax.ShapeDtypeStruct((16, D), BF16), in_...]
where the time goes in v6:
time: 102 us
  Pallas kernels  100 us (98%)
  local copies, waits for them, and re-layouts  1.67 us (2%)
    pallas_call x1, Pallas kernels, per_device(): pl.pallas_call(kernel, out_shape=jax.ShapeDtypeStruct((16, D), BF16), in_...  100 us

profile of v6, /device:TPU:1, one launch (start us, length us, event | category | flops | bytes accessed | tf_op | source)
XLA Modules:
  0.0 101.9 jit_solution(3626422232144341537)
XLA Ops:
  0.0 100.2 %attention_input_grad.1 = bf16[16,8192]{1,0:T(8,128)(2,1)} custom-call(bf16[256,8192]{1,0:T(8,128)(2,1)} %hid_hbm.1, f32[1,8192]{1,0:T(1,128)} %bitcast.3, bf16[256,256]{1,0:T(8,128)(2,1)} %wq_hbm.1, bf16[32,256]{1,0:T(8,128)(2,1)} %bitcast.4, bf16[32,256]{1,0:T(8,128)(2,1)} %bitcast.5, bf16[256,256]{1,0:T(8,128)(2,1)} %gc_hbm.1, ...), custom_call_target="tpu_custom_call" | custom-call | tf_op jit(solution)/shard_map/attention_input_grad/pallas_call | solution.py:716
  100.2 1.7 %copy.12 = bf16[16,8192]{1,0:T(8,128)(2,1)} copy(bf16[16,8192]{1,0:T(8,128)(2,1)} %attention_input_grad.1) | data formatting | bytes 524288
